TPU v7x, 32 devices: a whole 2x2x4 slice. The times are simulated.
32 devices in a mesh: dp: 2 (over x), row: 4 (over z), col: 4 (over y, core).
Axes of the slice: x: 2, y: 2, z: 4, core: 2. Of those that a mesh axis runs over, the one named last changes fastest.
Arguments:
- block_input: bfloat16 [32768, 896], P(('dp', 'row', 'col')), may hold values from -6 to 6
- first_gain: bfloat16 [896], P('col'), may hold values from 0.5 to 1.5
- joint_weight: bfloat16 [896, 1152], P('row', 'col'), may hold values from -0.1875 to 0.1875
- joint_bias: bfloat16 [1152], P('col'), may hold values from -3 to 3
- output_weight: bfloat16 [896, 896], P('row', 'col'), may hold values from -1 to 1
- second_gain: bfloat16 [896], P('col'), may hold values from 0.5 to 1.5
- gate_weight: bfloat16 [896, 4864], P('row', 'col'), may hold values from -0.1875 to 0.1875
- up_weight: bfloat16 [896, 4864], P('row', 'col'), may hold values from -0.1875 to 0.1875
- down_weight: bfloat16 [4864, 896], P('col', 'row'), may hold values from -0.078125 to 0.078125
- cotangent: bfloat16 [32768, 896], P(('dp', 'row', 'col')), may hold values from -6 to 6
Outputs:
- block_output: bfloat16 [32768, 896], P(('dp', 'row', 'col'))
- input_grad: bfloat16 [32768, 896], P(('dp', 'row', 'col'))
- first_gain_grad: float32 [896], P('col')
- joint_weight_grad: float32 [896, 1152], P('row', 'col')
- query_key_bias_grad: float32 [1024], P('col')
- value_bias_grad: float32 [128], P('col')
- output_weight_grad: float32 [896, 896], P('row', 'col')
- second_gain_grad: float32 [896], P('col')
- gate_weight_grad: float32 [896, 4864], P('row', 'col')
- up_weight_grad: float32 [896, 4864], P('row', 'col')
- down_weight_grad: float32 [4864, 896], P('col', 'row')
All inputs are finite; a program needn't handle non-finite values.
Results may differ from a plain program's by a relative error of at most 0.018.
Values may be sent and summed in bfloat16 or wider, within the bound.
No kernel may reach another device: no remote copies, remote signals or barrier semaphores. Data moves between devices by JAX's collectives and lax.ppermute only.
A program may use at most 256 MiB of HBM per device.

v0:
```python
import jax
import jax.numpy as jnp
from jax import lax
from jax.sharding import PartitionSpec as P

QH = 14
KVH = 2
HD = 64
SEQ_LEN = 1024


EPS = 1e-06
BASE = 1000000.0
MASKED = -1e30


def rotary_tables(length, head):
    half = head // 2
    freq = BASE ** (-(jnp.arange(half, dtype=jnp.float32) * 2.0 / head))
    angle = jnp.arange(length, dtype=jnp.float32)[:, None] * freq[None, :]
    return (jnp.cos(angle)[None, :, None, :], jnp.sin(angle)[None, :, None, :])


def rotate(values, cosine, sine):
    half = values.shape[-1] // 2
    first = values[..., :half]
    second = values[..., half:]
    return jnp.concatenate([first * cosine - second * sine, second * cosine + first * sine], -1)


def unrotate(values, cosine, sine):
    half = values.shape[-1] // 2
    first = values[..., :half]
    second = values[..., half:]
    return jnp.concatenate([first * cosine + second * sine, second * cosine - first * sine], -1)


def normalize(values, gain):
    inverse = lax.rsqrt(jnp.mean(values * values, -1, keepdims=True) + EPS)
    return (values * inverse * gain, inverse)


def normalize_back(values, inverse, gain, upstream):
    weighted = upstream * gain
    inner = jnp.mean(weighted * values, -1, keepdims=True)
    value_grad = inverse * weighted - values * inverse * inverse * inverse * inner
    gain_grad = jnp.sum(upstream * values * inverse, 0)
    return (value_grad, gain_grad)


def dot_left(left, right):
    return lax.dot_general(
        left, right, (((0,), (0,)), ((), ())), preferred_element_type=jnp.float32
    )


def dot_right(left, right):
    return lax.dot_general(
        left, right, (((1,), (1,)), ((), ())), preferred_element_type=jnp.float32
    )


def gate_back(gate, up_part, hidden_grad):
    sigma = jax.nn.sigmoid(gate)
    gate_grad = hidden_grad * up_part * sigma * (1.0 + gate * (1.0 - sigma))
    up_grad = hidden_grad * gate * sigma
    return (gate_grad.astype(jnp.bfloat16), up_grad.astype(jnp.bfloat16))


def causal(offset, rows, length):
    query_pos = offset + lax.broadcasted_iota(jnp.int32, (rows, length), 0)
    key_pos = lax.broadcasted_iota(jnp.int32, (rows, length), 1)
    return key_pos <= query_pos


def block_scores(query_block, key_head, offset):
    scale = query_block.shape[-1] ** (-0.5)
    scores = (
        jnp.einsum("qgd,ld->gql", query_block, key_head, preferred_element_type=jnp.float32) * scale
    )
    allowed = causal(offset, query_block.shape[0], key_head.shape[0])
    return jnp.where(allowed[None], scores, MASKED)


def block_forward(query_block, key_head, value_head, offset):
    scores = block_scores(query_block, key_head, offset)
    peak = jnp.max(scores, -1, keepdims=True)
    weights = jnp.exp(scores - peak)
    total = jnp.sum(weights, -1, keepdims=True)
    prob = (weights / total).astype(jnp.bfloat16)
    attended = jnp.einsum("gql,ld->qgd", prob, value_head, preferred_element_type=jnp.float32)
    return (attended.astype(jnp.bfloat16), peak + jnp.log(total))


def block_backward(query_block, key_head, value_head, grad_block, logsum, offset):
    scale = query_block.shape[-1] ** (-0.5)
    scores = block_scores(query_block, key_head, offset)
    prob = jnp.exp(scores - logsum)
    value_grad = jnp.einsum(
        "gql,qgd->ld", prob.astype(jnp.bfloat16), grad_block, preferred_element_type=jnp.float32
    )
    prob_grad = jnp.einsum(
        "qgd,ld->gql", grad_block, value_head, preferred_element_type=jnp.float32
    )
    inner = jnp.sum(prob * prob_grad, -1, keepdims=True)
    score_grad = (prob * (prob_grad - inner)).astype(jnp.bfloat16)
    query_grad = (
        jnp.einsum("gql,ld->qgd", score_grad, key_head, preferred_element_type=jnp.float32) * scale
    )
    key_grad = (
        jnp.einsum("gql,qgd->ld", score_grad, query_block, preferred_element_type=jnp.float32)
        * scale
    )
    return (query_grad, key_grad, value_grad)


def locate(index, blocks, kv_heads):
    seq = index // (blocks * kv_heads)
    block = index // kv_heads % blocks
    head = index % kv_heads
    return (seq, block, head)


def take_block(array, seq, start, head, rows):
    sizes = (1, rows, 1, array.shape[3], array.shape[4])
    return lax.dynamic_slice(array, (seq, start, head, 0, 0), sizes)[0, :, 0]


def take_head(array, seq, head):
    sizes = (1, array.shape[1], 1, array.shape[3])
    return lax.dynamic_slice(array, (seq, 0, head, 0), sizes)[0, :, 0]


def assemble(items, seq_count, blocks, kv_heads, rows):
    shaped = items.reshape(seq_count, blocks, kv_heads, rows, items.shape[2], items.shape[3])
    shaped = jnp.transpose(shaped, (0, 1, 3, 2, 4, 5))
    return shaped.reshape(seq_count * blocks * rows, kv_heads * items.shape[2] * items.shape[3])


def body(
    block_input,
    first_gain,
    joint_weight,
    joint_bias,
    output_weight,
    second_gain,
    gate_weight,
    up_weight,
    down_weight,
    cotangent,
):
    joint_rows, output_rows, gate_rows, up_rows, down_rows = (
        lax.all_gather(joint_weight, "row", axis=0, tiled=True),
        lax.all_gather(output_weight, "row", axis=0, tiled=True),
        lax.all_gather(gate_weight, "row", axis=0, tiled=True),
        lax.all_gather(up_weight, "row", axis=0, tiled=True),
        lax.all_gather(down_weight, "row", axis=1, tiled=True),
    )
    joint_full, output_full, first_full, second_full, bias_full, gate_full, up_full, down_full = (
        lax.all_gather(joint_rows, "col", axis=1, tiled=True),
        lax.all_gather(output_rows, "col", axis=1, tiled=True),
        lax.all_gather(first_gain, "col", axis=0, tiled=True),
        lax.all_gather(second_gain, "col", axis=0, tiled=True),
        lax.all_gather(joint_bias, "col", axis=0, tiled=True),
        lax.all_gather(gate_rows, "col", axis=1, tiled=True),
        lax.all_gather(up_rows, "col", axis=1, tiled=True),
        lax.all_gather(down_rows, "col", axis=0, tiled=True),
    )
    inputs = block_input.astype(jnp.float32)
    first_scale = first_full.astype(jnp.float32)
    second_scale = second_full.astype(jnp.float32)
    normed, first_inverse = normalize(inputs, first_scale)
    first_act = normed.astype(jnp.bfloat16)
    joint = jnp.dot(first_act, joint_full, preferred_element_type=jnp.float32) + bias_full.astype(
        jnp.float32
    )
    tokens = inputs.shape[0]
    seq_count = tokens // SEQ_LEN
    width = QH * HD
    kv_width = KVH * HD
    qk_width = width + kv_width
    group = QH // KVH
    cosine, sine = rotary_tables(SEQ_LEN, HD)
    queries = rotate(joint[:, :width].reshape(seq_count, SEQ_LEN, QH, HD), cosine, sine)
    queries = queries.astype(jnp.bfloat16).reshape(seq_count, SEQ_LEN, KVH, group, HD)
    key_rows = rotate(
        joint[:, width : width + kv_width].reshape(seq_count, SEQ_LEN, KVH, HD), cosine, sine
    ).astype(jnp.bfloat16)
    value_rows = (
        joint[:, width + kv_width :].reshape(seq_count, SEQ_LEN, KVH, HD).astype(jnp.bfloat16)
    )
    rows = min(512, SEQ_LEN)
    blocks = SEQ_LEN // rows
    order = jnp.arange(seq_count * blocks * KVH, dtype=jnp.int32)

    def forward_item(index):
        seq, block, head = locate(index, blocks, KVH)
        query_block = take_block(queries, seq, block * rows, head, rows)
        return block_forward(
            query_block,
            take_head(key_rows, seq, head),
            take_head(value_rows, seq, head),
            block * rows,
        )

    attended_items, logsums = lax.map(forward_item, order)
    attended = assemble(attended_items, seq_count, blocks, KVH, rows)
    resid = inputs + jnp.dot(attended, output_full, preferred_element_type=jnp.float32)
    normed_two, second_inverse = normalize(resid, second_scale)
    second_act = normed_two.astype(jnp.bfloat16)
    gate = jnp.dot(second_act, gate_full, preferred_element_type=jnp.float32)
    up_part = jnp.dot(second_act, up_full, preferred_element_type=jnp.float32)
    hidden = (jax.nn.silu(gate) * up_part).astype(jnp.bfloat16)
    mixed = jnp.dot(hidden, down_full, preferred_element_type=jnp.float32)
    hidden_grad = dot_right(cotangent, down_full)
    down_w_grad = dot_left(hidden, cotangent)
    gate_grad, up_grad = gate_back(gate, up_part, hidden_grad)
    gate_w_grad = dot_left(second_act, gate_grad)
    up_w_grad = dot_left(second_act, up_grad)
    second_grad = dot_right(gate_grad, gate_full) + dot_right(up_grad, up_full)
    block_output = (resid + mixed).astype(jnp.bfloat16)
    resid_norm_grad, second_gain_grad = normalize_back(
        resid, second_inverse, second_scale, second_grad
    )
    resid_grad = cotangent.astype(jnp.float32) + resid_norm_grad
    proj_grad = resid_grad.astype(jnp.bfloat16)
    output_w_grad = dot_left(attended, proj_grad)
    attended_grad = (
        dot_right(proj_grad, output_full)
        .astype(jnp.bfloat16)
        .reshape(seq_count, SEQ_LEN, KVH, group, HD)
    )

    def backward_item(index):
        seq, block, head = locate(index, blocks, KVH)
        query_block = take_block(queries, seq, block * rows, head, rows)
        grad_block = take_block(attended_grad, seq, block * rows, head, rows)
        return block_backward(
            query_block,
            take_head(key_rows, seq, head),
            take_head(value_rows, seq, head),
            grad_block,
            logsums[index],
            block * rows,
        )

    query_items, key_items, value_items = lax.map(backward_item, order)
    query_grad = assemble(query_items, seq_count, blocks, KVH, rows).reshape(
        seq_count, SEQ_LEN, QH, HD
    )
    query_grad = unrotate(query_grad, cosine, sine).reshape(tokens, width)
    key_grad = jnp.sum(key_items.reshape(seq_count, blocks, KVH, SEQ_LEN, HD), 1)
    key_grad = unrotate(jnp.transpose(key_grad, (0, 2, 1, 3)), cosine, sine).reshape(
        tokens, kv_width
    )
    value_grad = jnp.sum(value_items.reshape(seq_count, blocks, KVH, SEQ_LEN, HD), 1)
    value_grad = jnp.transpose(value_grad, (0, 2, 1, 3)).reshape(tokens, kv_width)
    joint_grad = jnp.concatenate([query_grad, key_grad, value_grad], 1).astype(jnp.bfloat16)
    joint_w_grad = dot_left(first_act, joint_grad)
    bias_grad = jnp.sum(joint_grad.astype(jnp.float32), 0)
    qk_bias_grad = bias_grad[:qk_width]
    value_b_grad = bias_grad[qk_width:]
    first_grad = dot_right(joint_grad, joint_full)
    input_norm_grad, first_gain_grad = normalize_back(
        inputs, first_inverse, first_scale, first_grad
    )
    input_grad = (resid_grad + input_norm_grad).astype(jnp.bfloat16)
    (
        joint_w_grad,
        output_w_grad,
        qk_bias_grad,
        value_b_grad,
        first_gain_grad,
        second_gain_grad,
        gate_w_grad,
        up_w_grad,
        down_w_grad,
    ) = (
        lax.psum_scatter(
            joint_w_grad.astype(jnp.bfloat16), "col", scatter_dimension=1, tiled=True
        ).astype(jnp.float32),
        lax.psum_scatter(
            output_w_grad.astype(jnp.bfloat16), "col", scatter_dimension=1, tiled=True
        ).astype(jnp.float32),
        lax.psum_scatter(
            qk_bias_grad.astype(jnp.bfloat16), "col", scatter_dimension=0, tiled=True
        ).astype(jnp.float32),
        lax.psum_scatter(
            value_b_grad.astype(jnp.bfloat16), "col", scatter_dimension=0, tiled=True
        ).astype(jnp.float32),
        lax.psum_scatter(
            first_gain_grad.astype(jnp.bfloat16), "col", scatter_dimension=0, tiled=True
        ).astype(jnp.float32),
        lax.psum_scatter(
            second_gain_grad.astype(jnp.bfloat16), "col", scatter_dimension=0, tiled=True
        ).astype(jnp.float32),
        lax.psum_scatter(
            gate_w_grad.astype(jnp.bfloat16), "col", scatter_dimension=1, tiled=True
        ).astype(jnp.float32),
        lax.psum_scatter(
            up_w_grad.astype(jnp.bfloat16), "col", scatter_dimension=1, tiled=True
        ).astype(jnp.float32),
        lax.psum_scatter(
            down_w_grad.astype(jnp.bfloat16), "col", scatter_dimension=0, tiled=True
        ).astype(jnp.float32),
    )
    joint_w_grad, output_w_grad, gate_w_grad, up_w_grad, down_w_grad = (
        lax.psum_scatter(
            joint_w_grad.astype(jnp.bfloat16), "row", scatter_dimension=0, tiled=True
        ).astype(jnp.float32),
        lax.psum_scatter(
            output_w_grad.astype(jnp.bfloat16), "row", scatter_dimension=0, tiled=True
        ).astype(jnp.float32),
        lax.psum_scatter(
            gate_w_grad.astype(jnp.bfloat16), "row", scatter_dimension=0, tiled=True
        ).astype(jnp.float32),
        lax.psum_scatter(
            up_w_grad.astype(jnp.bfloat16), "row", scatter_dimension=0, tiled=True
        ).astype(jnp.float32),
        lax.psum_scatter(
            down_w_grad.astype(jnp.bfloat16), "row", scatter_dimension=1, tiled=True
        ).astype(jnp.float32),
    )
    joint_w_grad, output_w_grad, gate_w_grad, up_w_grad, down_w_grad = (
        lax.psum(joint_w_grad.astype(jnp.bfloat16), "dp").astype(jnp.float32),
        lax.psum(output_w_grad.astype(jnp.bfloat16), "dp").astype(jnp.float32),
        lax.psum(gate_w_grad.astype(jnp.bfloat16), "dp").astype(jnp.float32),
        lax.psum(up_w_grad.astype(jnp.bfloat16), "dp").astype(jnp.float32),
        lax.psum(down_w_grad.astype(jnp.bfloat16), "dp").astype(jnp.float32),
    )
    qk_bias_grad, value_b_grad, first_gain_grad, second_gain_grad = lax.psum(
        (qk_bias_grad, value_b_grad, first_gain_grad, second_gain_grad), ("dp", "row")
    )
    return (
        block_output,
        input_grad,
        first_gain_grad,
        joint_w_grad,
        qk_bias_grad,
        value_b_grad,
        output_w_grad,
        second_gain_grad,
        gate_w_grad,
        up_w_grad,
        down_w_grad,
    )


def solution(mesh):
    return jax.shard_map(
        body,
        mesh=mesh,
        in_specs=(
            P(("dp", "row", "col"), None),
            P("col"),
            P("row", "col"),
            P("col"),
            P("row", "col"),
            P("col"),
            P("row", "col"),
            P("row", "col"),
            P("col", "row"),
            P(("dp", "row", "col"), None),
        ),
        out_specs=(
            P(("dp", "row", "col"), None),
            P(("dp", "row", "col"), None),
            P("col"),
            P("row", "col"),
            P("col"),
            P("col"),
            P("row", "col"),
            P("col"),
            P("row", "col"),
            P("row", "col"),
            P("col", "row"),
        ),
        check_vma=False,
    )
```

profile of v0, /device:TPU:0, one launch (start us, length us, event | category | flops | bytes accessed | tf_op | source)
XLA Modules:
  0.0 1229.2 jit_solution(4716211249559498046)
XLA Ops:
  8.7 21.8 %all-gather = bf16[4,224,288]{1,2,0:T(8,128)(2,1)S(1)} all-gather(bf16[1,224,288]{1,2,0:T(8,128)(2,1)} %bitcast.255), channel_id=1, replica_groups=mesh['dp'=2,'row'=4,'col'=4] {'row'}, dimensions={0}, use_global_device_ids=true | all-gather | bytes 645120 | tf_op jit(solution)/shard_map/all_gather | solution.py:153
  32.9 20.6 %all_gather.43 = bf16[896,224]{1,0:T(8,128)(2,1)S(1)} all-gather(bf16[224,224]{1,0:T(8,128)(2,1)S(1)} %copy-done.18), channel_id=1, replica_groups=mesh['dp'=2,'row'=4,'col'=4] {'row'}, dimensions={0}, use_global_device_ids=true | all-gather | bytes 501760 | tf_op jit(solution)/shard_map/all_gather | solution.py:154
  54.5 16.7 %all-gather.14.cloned.1.call-done = bf16[896,1216]{1,0:T(8,128)(2,1)} async-done(((bf16[224,1216]{1,0:T(8,128)(2,1)}), bf16[896,1216]{1,0:T(8,128)(2,1)}) %all-gather.14.cloned.1.call-update) | async-done | bytes 2179088 | tf_op jit(solution)/shard_map/all_gather | solution.py:155
  75.6 45.8 %all-gather.18.cloned.1.call-done = bf16[896,1216]{1,0:T(8,128)(2,1)} async-done(((bf16[224,1216]{1,0:T(8,128)(2,1)}), bf16[896,1216]{1,0:T(8,128)(2,1)}) %all-gather.18.cloned.1.call-update) | async-done | bytes 2179088 | tf_op jit(solution)/shard_map/all_gather | solution.py:156
  161.7 34.0 %all-gather.22.cloned.1.call-done = bf16[1216,896]{0,1:T(8,128)(2,1)} async-done(((bf16[1216,224]{0,1:T(8,128)(2,1)}), bf16[1216,896]{0,1:T(8,128)(2,1)}) %all-gather.22.cloned.1.call-update) | async-done | bytes 2179088 | tf_op jit(solution)/shard_map/all_gather | solution.py:157
  200.3 111.3 %while.30 = (s32[]{:T(128)}, bf16[4,512,7,64]{1,3,2,0:T(8,128)(2,1)}, f32[4,7,512,1]{2,1,3,0:T(8,128)}, s32[4]{0:T(128)S(1)}, bf16[1,1024,2,64]{1,3,2,0:T(8,128)...) while((s32[]{:T(128)}, ...), condition=%wide.region_4.5_spmd, body=%wide.region_1.4_spmd.sunk | while | flops 984314880 | bytes 47445000 | solution.py:206
  219.4 8.8 fusion.126
  274.8 8.4 fusion.126
  324.8 18.2 %fusion.76 = f32[1024,4864]{1,0:T(8,128)} fusion(bf16[1024,896]{0,1:T(8,128)(2,1)} %multiply_convert_fusion.3, bf16[896,4864]{0,1:T(8,128)(2,1)} %all-gather.16.cloned.1.call-done), kind=kOutput, calls=%fused_computation.132 | convolution fusion | flops 8925478912 | bytes 30474240 | tf_op jit(solution)/shard_map/dot_general | solution.py:211
  343.0 17.8 %fusion.77 = f32[1024,4864]{1,0:T(8,128)} fusion(bf16[1024,896]{0,1:T(8,128)(2,1)} %multiply_convert_fusion.3, bf16[896,4864]{0,1:T(8,128)(2,1)} %all-gather.20.cloned.1.call-done), kind=kOutput, calls=%fused_computation.133 | convolution fusion | flops 8925478912 | bytes 30474240 | tf_op jit(solution)/shard_map/dot_general | solution.py:212
  360.7 40.2 %all-gather.24.cloned.1.call-done = bf16[4864,896]{1,0:T(8,128)(2,1)} async-done(((bf16[1216,896]{1,0:T(8,128)(2,1)}), bf16[4864,896]{1,0:T(8,128)(2,1)}) %all-gather.24.cloned.1.call-update) | async-done | bytes 8716304 | tf_op jit(solution)/shard_map/all_gather | solution.py:167
  400.9 31.7 %multiply_convert_fusion = (bf16[1024,4864]{1,0:T(8,128)(2,1)}, bf16[1024,4864]{1,0:T(8,128)(2,1)}, bf16[1024,4864]{1,0:T(8,128)(2,1)}) fusion(f32[1024,4864]{1,0:T(8,128)} %fusion.76, f32[1024,4864]{1,0:T(8,128)} %fusion.77, bf16[1024,896]{1,0:T(8,128)(2,1)} %param.23, bf16[4864,896]{1,0:T(8,128)(2,1)} %all-gather.24.cloned.1.call-done), kind=kOutput, calls=%fused_computation.65 | convolution fusion | flops 9005170688 | bytes 80281600 | tf_op jit(solution)/shard_map/dot_general | solution.py:58
  432.7 15.6 %fusion.78 = f32[1024,896]{0,1:T(8,128)} fusion(bf16[1024,4864]{1,0:T(8,128)(2,1)} %get-tuple-element.359, bf16[896,4864]{0,1:T(8,128)(2,1)} %all-gather.16.cloned.1.call-done), kind=kOutput, calls=%fused_computation.134 | convolution fusion | flops 8925478912 | bytes 22347776 | tf_op jit(solution)/shard_map/dot_general | solution.py:58
  448.3 18.9 %multiply_reduce_fusion = (bf16[896]{0:T(1024)(128)(2,1)}, f32[1024]{0:T(1024)S(1)}, f32[1024,896]{0,1:T(8,128)}) fusion(f32[1024,896]{0,1:T(8,128)} %copy-done.5, f32[1024]{0:T(1024)S(1)} %add_rsqrt_fusion, f32[896]{0:T(1024)S(1)} %copy-done.20, f32[1024,896]{0,1:T(8,128)} %fusion.78, bf16[1024,4864]{1,0:T(8,128)(2,1)} %get-tuple-element.358, ...), kind=kOutput, calls=%fused_computation.91 | convolution fusion | flops 8931899392 | bytes 29701376 | tf_op jit(solution)/shard_map/dot_general | solution.py:58
  483.2 187.3 %while.31 = (s32[]{:T(128)}, f32[4,512,7,64]{1,3,2,0:T(8,128)}, f32[4,1024,64]{1,2,0:T(8,128)}, f32[4,1024,64]{1,2,0:T(8,128)}, s32[4]{0:T(128)S(1)}, /*index=5*...) while((s32[]{:T(128)}, f32[4,512,7,64]{1,3,2,0:T(8,128)}, ...), condition=%wide.region_9.10_spmd, body=%wide.region_7.9_spmd.sunk | while | flops 2382656512 | bytes 232342768 | solution.py:247
  497.7 12.8 %fusion.136 = (f32[7,512]{1,0:T(8,128)S(1)}, f32[7,512,1024]{1,2,0:T(8,128)}) fusion(f32[1024,512,7]{1,0,2:T(8,128)} %fusion.135, f32[7,512]{1,0:T(8,128)S(1)} %dynamic-slice_bitcast_fusion.2, bf16[1,1024,2,7,64]{1,4,3,2,0:T(8,128)(2,1)S(1)} %get-tuple-element.570, s32[]{:T(128)S(6)} %select_n.149, s32[]{:T(128)S(6)} %select_n.151, ...), kind=kOutput, calls=%fused_computation.25.clone.1 | convolution fusion | flops 488108544 | bytes 30506496 | tf_op jit(solution)/shard_map/while/body/eval_jaxpr/qgd,ld->gql/dot_general | solution.py:79
  544.5 12.7 %fusion.136 = (f32[7,512]{1,0:T(8,128)S(1)}, f32[7,512,1024]{1,2,0:T(8,128)}) fusion(f32[1024,512,7]{1,0,2:T(8,128)} %fusion.135, f32[7,512]{1,0:T(8,128)S(1)} %dynamic-slice_bitcast_fusion.2, bf16[1,1024,2,7,64]{1,4,3,2,0:T(8,128)(2,1)S(1)} %get-tuple-element.570, s32[]{:T(128)S(6)} %select_n.149, s32[]{:T(128)S(6)} %select_n.151, ...), kind=kOutput, calls=%fused_computation.25.clone.1 | convolution fusion | flops 488108544 | bytes 30506496 | tf_op jit(solution)/shard_map/while/body/eval_jaxpr/qgd,ld->gql/dot_general | solution.py:79
  591.2 12.7 %fusion.136 = (f32[7,512]{1,0:T(8,128)S(1)}, f32[7,512,1024]{1,2,0:T(8,128)}) fusion(f32[1024,512,7]{1,0,2:T(8,128)} %fusion.135, f32[7,512]{1,0:T(8,128)S(1)} %dynamic-slice_bitcast_fusion.2, bf16[1,1024,2,7,64]{1,4,3,2,0:T(8,128)(2,1)S(1)} %get-tuple-element.570, s32[]{:T(128)S(6)} %select_n.149, s32[]{:T(128)S(6)} %select_n.151, ...), kind=kOutput, calls=%fused_computation.25.clone.1 | convolution fusion | flops 488108544 | bytes 30506496 | tf_op jit(solution)/shard_map/while/body/eval_jaxpr/qgd,ld->gql/dot_general | solution.py:79
  637.8 12.7 %fusion.136 = (f32[7,512]{1,0:T(8,128)S(1)}, f32[7,512,1024]{1,2,0:T(8,128)}) fusion(f32[1024,512,7]{1,0,2:T(8,128)} %fusion.135, f32[7,512]{1,0:T(8,128)S(1)} %dynamic-slice_bitcast_fusion.2, bf16[1,1024,2,7,64]{1,4,3,2,0:T(8,128)(2,1)S(1)} %get-tuple-element.570, s32[]{:T(128)S(6)} %select_n.149, s32[]{:T(128)S(6)} %select_n.151, ...), kind=kOutput, calls=%fused_computation.25.clone.1 | convolution fusion | flops 488108544 | bytes 30506496 | tf_op jit(solution)/shard_map/while/body/eval_jaxpr/qgd,ld->gql/dot_general | solution.py:79
  693.4 15.8 %convolution_convert_fusion.2 = bf16[4864,896]{1,0:T(8,128)(2,1)} fusion(bf16[1024,4864]{1,0:T(8,128)(2,1)} %get-tuple-element.360, bf16[1024,896]{1,0:T(8,128)(2,1)} %param.23), kind=kOutput, calls=%fused_computation.71 | convolution fusion | flops 8929837056 | bytes 20512768 | tf_op jit(solution)/shard_map/dot_general | solution.py:52
  709.2 16.4 %convolution_convert_fusion.1 = bf16[896,4864]{0,1:T(8,128)(2,1)} fusion(bf16[1024,896]{0,1:T(8,128)(2,1)} %multiply_convert_fusion.3, bf16[1024,4864]{1,0:T(8,128)(2,1)} %get-tuple-element.359), kind=kOutput, calls=%fused_computation.70 | convolution fusion | flops 8929837056 | bytes 20512768 | tf_op jit(solution)/shard_map/dot_general | solution.py:52
  725.7 16.2 %convolution_convert_fusion = bf16[896,4864]{0,1:T(8,128)(2,1)} fusion(bf16[1024,896]{0,1:T(8,128)(2,1)} %multiply_convert_fusion.3, bf16[1024,4864]{1,0:T(8,128)(2,1)} %get-tuple-element.358), kind=kOutput, calls=%fused_computation.69 | convolution fusion | flops 8929837056 | bytes 20512768 | tf_op jit(solution)/shard_map/dot_general | solution.py:52
  746.3 54.8 %reduce-scatter.29.cloned.1.call-done = bf16[1216,896]{1,0:T(8,128)(2,1)} async-done(((bf16[4864,896]{1,0:T(8,128)(2,1)}), bf16[1216,896]{1,0:T(8,128)(2,1)}) %reduce-scatter.29.cloned.1.call-update) | async-done | bytes 2179088 | tf_op jit(solution)/shard_map/reduce_scatter | solution.py:303
  805.4 72.0 %reduce-scatter.25.cloned.1.call-done = bf16[896,1216]{0,1:T(8,128)(2,1)} async-done(((bf16[896,4864]{0,1:T(8,128)(2,1)}), bf16[896,1216]{0,1:T(8,128)(2,1)}) %reduce-scatter.25.cloned.1.call-update) | async-done | bytes 2179088 | tf_op jit(solution)/shard_map/reduce_scatter | solution.py:297
  881.9 71.9 %reduce-scatter.27.cloned.1.call-done = bf16[896,1216]{0,1:T(8,128)(2,1)} async-done(((bf16[896,4864]{0,1:T(8,128)(2,1)}), bf16[896,1216]{0,1:T(8,128)(2,1)}) %reduce-scatter.27.cloned.1.call-update) | async-done | bytes 2179088 | tf_op jit(solution)/shard_map/reduce_scatter | solution.py:300
  979.2 22.2 %reduce-scatter.31.cloned.1.call-done = bf16[224,288]{1,0:T(8,128)(2,1)} async-done(((bf16[896,288]{1,0:T(8,128)(2,1)}), bf16[224,288]{1,0:T(8,128)(2,1)}) %reduce-scatter.31.cloned.1.call-update) | async-done | bytes 129040
  1003.0 46.4 %reduce-scatter.39.cloned.1.call-done = bf16[224,1216]{1,0:T(8,128)(2,1)} async-done(((bf16[896,1216]{1,0:T(8,128)(2,1)}), bf16[224,1216]{1,0:T(8,128)(2,1)}) %reduce-scatter.39.cloned.1.call-update) | async-done | bytes 544784
  1051.6 46.7 %reduce-scatter.35.cloned.1.call-done = bf16[224,1216]{1,0:T(8,128)(2,1)} async-done(((bf16[896,1216]{1,0:T(8,128)(2,1)}), bf16[224,1216]{1,0:T(8,128)(2,1)}) %reduce-scatter.35.cloned.1.call-update) | async-done | bytes 544784
  1100.4 46.6 %reduce-scatter.37.cloned.1.call-done = bf16[224,1216]{1,0:T(8,128)(2,1)} async-done(((bf16[896,1216]{1,0:T(8,128)(2,1)}), bf16[224,1216]{1,0:T(8,128)(2,1)}) %reduce-scatter.37.cloned.1.call-update) | async-done | bytes 544784
  1149.1 15.0 %add_convert_fusion = bf16[1024,896]{0,1:T(8,128)(2,1)S(1)} fusion(f32[1024,896]{0,1:T(8,128)} %copy-done.5, bf16[1024,4864]{1,0:T(8,128)(2,1)} %get-tuple-element.360, bf16[4864,896]{1,0:T(8,128)(2,1)} %all-gather.24.cloned.1.call-done), kind=kOutput, calls=%fused_computation.94 | convolution fusion | flops 8927313920 | bytes 24182784 | tf_op jit(solution)/shard_map/dot_general | solution.py:214
  1173.7 20.8 %all-reduce.7 = (f32[224]{0:T(256)}, f32[256]{0:T(256)}, f32[32]{0:T(128)}, f32[224]{0:T(256)}) all-reduce(f32[224]{0:T(256)S(1)} %get-tuple-element.378, f32[256]{0:T(256)S(1)} %dynamic-slice_convert_fusion.2, f32[32]{0:T(128)S(1)} %dynamic-slice_convert_fusion.1, ...), channel_id=1, replica_groups=mesh['dp'=2,'row'=4,'col'=4] {'dp','row'}, use_global_device_ids=true, to_apply=%region_15.16 | all-reduce | flops 736 | bytes 5888 | tf_op jit(solution)/shard_map/psum | solution.py:331
  1194.5 20.3 %all-reduce.13.cloned.1.call-done = (bf16[224,224]{0,1:T(8,128)(2,1)}, bf16[224,1216]{0,1:T(8,128)(2,1)}, bf16[224,1216]{0,1:T(8,128)(2,1)}, bf16[1216,224]{1,0:T(8,128)(2,1)}, bf16[224,288]{0,1:T(8,128)(2,1)}) async-done(((bf16[224,224]{0,1:T(8,128)(2,1)}, bf16[224,1216]{0,1:T(8,128)(2,1)}, bf16[224,1216]{0,1:T(8,128)(2,1)}, bf16[1216,224]{1,0:T(8,128)(2,1)}, bf16[224,288]{0,1:T(8,128)(2,1)}), ...) | async-done | bytes 1863696 | tf_op jit(solution)/shard_map/psum | solution.py:326
  (311 shorter events, 369.3 us)
Async XLA Ops:
  7.2 25.7 %copy-start.18 = (bf16[224,224]{1,0:T(8,128)(2,1)S(1)}, bf16[224,224]{1,0:T(8,128)(2,1)}, u32[]{:S(2)}) copy-start(bf16[224,224]{1,0:T(8,128)(2,1)} %param.18) | copy-start | bytes 301060
  7.2 64.0 %all-gather.14.cloned.1.call-start = ((), (), s32[]{:S(2)}) async-start(), calls=%async_computation.12 | async-start | bytes 2867200 | tf_op jit(solution)/shard_map/all_gather | solution.py:155
  7.9 113.5 %all-gather.18.cloned.1.call-start = ((), (), s32[]{:S(2)}) async-start(), calls=%async_computation.14 | async-start | bytes 2867200 | tf_op jit(solution)/shard_map/all_gather | solution.py:156
  8.7 136.4 %all-gather.10.cloned.1.call-start = ((), (), s32[]{:S(2)}) async-start(), calls=%async_computation.10 | async-start | bytes 2580480 | tf_op jit(solution)/shard_map/all_gather | solution.py:160
  32.3 163.5 %all-gather.22.cloned.1.call-start = ((), (), s32[]{:S(2)}) async-start(), calls=%async_computation.16 | async-start | bytes 2867200 | tf_op jit(solution)/shard_map/all_gather | solution.py:157
  32.9 283.8 %all-gather.12.cloned.1.call-start = ((), (), s32[]{:S(2)}) async-start(), calls=%async_computation.11 | async-start | bytes 2007040 | tf_op jit(solution)/shard_map/all_gather | solution.py:161
  54.5 270.3 %all-gather.16.cloned.1.call-start = ((), (), s32[]{:S(2)}) async-start(), calls=%async_computation.13 | async-start | bytes 10895360 | tf_op jit(solution)/shard_map/all_gather | solution.py:165
  75.5 50.3 %copy-start.26 = (u32[32]{0:T(128)S(1)}, u32[32]{0:T(128)}, u32[]{:S(2)}) copy-start(u32[32]{0:T(128)} %constant.227) | copy-start | bytes 388
  75.5 52.2 %copy-start.29 = (bf16[224]{0:T(256)(128)(2,1)S(1)}, bf16[224]{0:T(256)(128)(2,1)}, u32[]{:S(2)}) copy-start(bf16[224]{0:T(256)(128)(2,1)} %param.15) | copy-start | bytes 1348
  75.5 52.4 %copy-start.30 = (bf16[224]{0:T(256)(128)(2,1)S(1)}, bf16[224]{0:T(256)(128)(2,1)}, u32[]{:S(2)}) copy-start(bf16[224]{0:T(256)(128)(2,1)} %param.19) | copy-start | bytes 1348
  75.5 52.7 %copy-start.28 = (bf16[288]{0:T(512)(128)(2,1)S(1)}, bf16[288]{0:T(512)(128)(2,1)}, u32[]{:S(2)}) copy-start(bf16[288]{0:T(512)(128)(2,1)} %param.17) | copy-start | bytes 1732
  75.5 267.4 %all-gather.20.cloned.1.call-start = ((), (), s32[]{:S(2)}) async-start(), calls=%async_computation.15 | async-start | bytes 10895360 | tf_op jit(solution)/shard_map/all_gather | solution.py:166
  125.7 275.3 %all-gather.24.cloned.1.call-start = ((), (), s32[]{:S(2)}) async-start(), calls=%async_computation.17 | async-start | bytes 10895360 | tf_op jit(solution)/shard_map/all_gather | solution.py:167
  144.2 14.6 %copy-start.10 = (f32[1024,32]{0,1:T(8,128)}, f32[1024,32]{0,1:T(8,128)S(1)}, u32[]{:S(2)}) copy-start(f32[1024,32]{0,1:T(8,128)S(1)} %get-tuple-element.371) | copy-start | bytes 393220
  144.2 14.6 %copy-start.12 = (f32[1024,32]{0,1:T(8,128)}, f32[1024,32]{0,1:T(8,128)S(1)}, u32[]{:S(2)}) copy-start(f32[1024,32]{0,1:T(8,128)S(1)} %get-tuple-element.372) | copy-start | bytes 393220
  200.0 542.0 %reduce-scatter.23.cloned.1.call-start = ((), (), s32[]{:S(2)}) async-start(), calls=%async_computation.19 | async-start | bytes 2007040 | tf_op jit(solution)/shard_map/reduce_scatter | solution.py:282
  477.3 266.8 %reduce-scatter.21.cloned.1.call-start = ((), (), s32[]{:S(2)}) async-start(), calls=%async_computation.18 | async-start | bytes 2580480 | tf_op jit(solution)/shard_map/reduce_scatter | solution.py:279
  483.6 14.1 %copy-start.1 = (bf16[1,1024,2,7,64]{1,4,3,2,0:T(8,128)(2,1)}, bf16[1,1024,2,7,64]{1,4,3,2,0:T(8,128)(2,1)S(1)}, u32[]{:S(2)}) copy-start(bf16[1,1024,2,7,64]{1,4,3,2,0:T(8,128)(2,1)S(1)} %get-tuple-element.570) | copy-start | bytes 5505028 | tf_op jit(solution)/shard_map/while
  497.7 14.0 %slice-start.2 = ((s8[14680064]{0:T(1024)(128)(4,1)}), s8[4194304]{0:T(1024)(128)(4,1)S(1)}, s32[]{:S(2)}) async-start(s8[14680064]{0:T(1024)(128)(4,1)} %bitcast.229), calls=%async_computation.31 | async-start | bytes 8388608 | tf_op jit(solution)/shard_map/while
  497.7 14.6 %slice-start.3 = ((s8[14680064]{0:T(1024)(128)(4,1)}), s8[2097152]{0:T(1024)(128)(4,1)S(1)}, s32[]{:S(2)}) async-start(s8[14680064]{0:T(1024)(128)(4,1)} %bitcast.229), calls=%async_computation.32 | async-start | bytes 4194304 | tf_op jit(solution)/shard_map/while
  544.5 14.5 %slice-start.3 = ((s8[14680064]{0:T(1024)(128)(4,1)}), s8[2097152]{0:T(1024)(128)(4,1)S(1)}, s32[]{:S(2)}) async-start(s8[14680064]{0:T(1024)(128)(4,1)} %bitcast.229), calls=%async_computation.32 | async-start | bytes 4194304 | tf_op jit(solution)/shard_map/while
  591.2 14.5 %slice-start.3 = ((s8[14680064]{0:T(1024)(128)(4,1)}), s8[2097152]{0:T(1024)(128)(4,1)S(1)}, s32[]{:S(2)}) async-start(s8[14680064]{0:T(1024)(128)(4,1)} %bitcast.229), calls=%async_computation.32 | async-start | bytes 4194304 | tf_op jit(solution)/shard_map/while
  637.8 14.5 %slice-start.3 = ((s8[14680064]{0:T(1024)(128)(4,1)}), s8[2097152]{0:T(1024)(128)(4,1)S(1)}, s32[]{:S(2)}) async-start(s8[14680064]{0:T(1024)(128)(4,1)} %bitcast.229), calls=%async_computation.32 | async-start | bytes 4194304 | tf_op jit(solution)/shard_map/while
  693.3 107.8 %reduce-scatter.29.cloned.1.call-start = ((), (), s32[]{:S(2)}) async-start(), calls=%async_computation.22 | async-start | bytes 10895360 | tf_op jit(solution)/shard_map/reduce_scatter | solution.py:303
  709.2 168.2 %reduce-scatter.25.cloned.1.call-start = ((), (), s32[]{:S(2)}) async-start(), calls=%async_computation.20 | async-start | bytes 10895360 | tf_op jit(solution)/shard_map/reduce_scatter | solution.py:297
  725.6 228.2 %reduce-scatter.27.cloned.1.call-start = ((), (), s32[]{:S(2)}) async-start(), calls=%async_computation.21 | async-start | bytes 10895360 | tf_op jit(solution)/shard_map/reduce_scatter | solution.py:300
  741.9 235.6 %reduce-scatter.33.cloned.1.call-start = ((), (), s32[]{:S(2)}) async-start(), calls=%async_computation.24 | async-start | bytes 573440
  744.0 257.3 %reduce-scatter.31.cloned.1.call-start = ((), (), s32[]{:S(2)}) async-start(), calls=%async_computation.23 | async-start | bytes 860160
  746.3 303.2 %reduce-scatter.39.cloned.1.call-start = ((), (), s32[]{:S(2)}) async-start(), calls=%async_computation.27 | async-start | bytes 2867200
  805.4 292.9 %reduce-scatter.35.cloned.1.call-start = ((), (), s32[]{:S(2)}) async-start(), calls=%async_computation.25 | async-start | bytes 2867200
  881.8 265.1 %reduce-scatter.37.cloned.1.call-start = ((), (), s32[]{:S(2)}) async-start(), calls=%async_computation.26 | async-start | bytes 2867200
  958.0 256.8 %all-reduce.13.cloned.1.call-start = ((), (), s32[]{:S(2)}) async-start(), calls=%async_computation.28 | async-start | bytes 4259840 | tf_op jit(solution)/shard_map/psum | solution.py:326
  (45 other events, 352.2 us)
Sparse Core Ops, SparseCore 0:
  9.6 61.5 all-gather.13
  72.8 48.5 all-gather.17
  123.5 21.4 all-gather.9
  146.5 49.2 all-gather.21
  197.2 18.6 all-gather.11
  217.3 60.1 all-gather.15
  279.0 60.1 all-gather.19
  340.8 60.1 all-gather.23
  477.4 28.4 reduce-scatter.22
  693.4 31.2 reduce-scatter.20
  727.4 73.7 reduce-scatter.28
  803.6 73.7 reduce-scatter.24
  880.0 73.7 reduce-scatter.26
  956.5 20.9 reduce-scatter.32
  980.3 20.9 reduce-scatter.30
  1003.5 45.8 reduce-scatter.38
  1051.7 46.4 reduce-scatter.34
  1100.4 46.4 reduce-scatter.36
  1150.8 63.9 all-reduce.12
where the time goes:
time: 1240 us; the launch traced here: 1230 us
  waiting for transfers between devices  524 us (42%)
  matrix products  385 us (31%)
  local copies, waits for them, and re-layouts  110 us (9%)
  other arithmetic  86.5 us (7%)
  blocking collectives  77.5 us (6%)
  loops' own time  27.1 us (2%)
  between operations  18.3 us (1%)
    unnamed x24, waiting for transfers between devices  168 us
    dot_general x8, matrix products, block_scores(): jnp.einsum('qgd,ld->gql', query_block, key_head, preferred_element_type=j...  78.4 us
    dot_general x5, matrix products, dot_right(): lax.dot_general(left, right, (((1,), (1,)), ((), ())), preferred_element_...  77.8 us
    reduce_scatter x1, waiting for transfers between devices, body(): lax.psum_scatter(gate_w_grad.astype(jnp.bfloat16), 'col', scatter_dimensi...  72 us
    reduce_scatter x1, waiting for transfers between devices, body(): lax.psum_scatter(up_w_grad.astype(jnp.bfloat16), 'col', scatter_dimension...  71.9 us
    unnamed x83, local copies, waits for them, and re-layouts  56.6 us
    dot_general x5, matrix products, dot_left(): lax.dot_general(left, right, (((0,), (0,)), ((), ())), preferred_element_...  55.8 us
    reduce_scatter x1, waiting for transfers between devices, body(): lax.psum_scatter(down_w_grad.astype(jnp.bfloat16), 'col', scatter_dimensi...  54.8 us
  transfers between devices with their start and end apart: 19, of which 14 were waited for; matrix products, arithmetic and copies ran while one was open for 39% of the time, Pallas kernels for 0%

commit v1 on v0

v1 whole, which is shorter than its diff:
```python
import functools

import jax
import jax.numpy as jnp
from jax import lax
from jax.experimental import pallas as pl
from jax.experimental.pallas import tpu as pltpu
from jax.sharding import PartitionSpec as P

QH = 14
KVH = 2
HD = 64
SEQ_LEN = 1024
GROUP = QH // KVH
WIDTH = QH * HD
KV_WIDTH = KVH * HD
QK_WIDTH = WIDTH + KV_WIDTH
QKV = QK_WIDTH + KV_WIDTH

EPS = 1e-06
BASE = 1000000.0
MASKED = -1e30
LANES = 128
BLOCK = 256

NN = (((1,), (0,)), ((), ()))
NT = (((1,), (1,)), ((), ()))
TN = (((0,), (0,)), ((), ()))
VMEM_BYTES = 56 * 1024 * 1024


def dot(left, right, dims=NN):
    return lax.dot_general(left, right, dims, preferred_element_type=jnp.float32)


def low(values):
    return values.astype(jnp.bfloat16)


def add(left, right):
    return low(left.astype(jnp.float32) + right.astype(jnp.float32))


def cost(flops, moved, transcendentals=0):
    return pl.CostEstimate(
        flops=int(flops), bytes_accessed=int(moved), transcendentals=int(transcendentals)
    )


def flip(values, axis, size, bit):
    return lax.ppermute(values, axis, [(i, i ^ bit) for i in range(size)])


def shift(values, axis, size):
    return lax.ppermute(values, axis, [(i, (i + 1) % size) for i in range(size)])


def join(mine, other, odd, axis):
    first = jnp.where(odd, other, mine)
    second = jnp.where(odd, mine, other)
    return jnp.concatenate([first, second], axis)


def half_of(values, which, axis):
    size = values.shape[axis] // 2
    return lax.dynamic_slice_in_dim(values, which * size, size, axis)


def after(values, done):
    return lax.optimization_barrier((values, done))[0]


class Grid:
    def __init__(self, sizes):
        self.dp, self.row, self.col = sizes["dp"], sizes["row"], sizes["col"]
        self.at_dp = lax.axis_index("dp")
        self.at_row = lax.axis_index("row")
        self.at_col = lax.axis_index("col")
        self.odd_dp = self.at_dp % 2
        self.core = self.at_col % 2
        self.pair = self.at_col // 2

    def gather_rows(self, block, axis, holds=()):
        size = block.shape[axis]
        mine = half_of(block, self.odd_dp, axis)
        shape = list(block.shape)
        shape[axis] = size * self.row
        full = jnp.zeros(shape, block.dtype)
        full = lax.dynamic_update_slice_in_dim(full, block, self.at_row * size, axis)
        for step in range(1, self.row):
            mine = shift(mine, "row", self.row)
            if holds:
                mine = after(mine, holds[step - 1])
            other = flip(mine, "dp", self.dp, 1)
            if holds:
                other = after(other, holds[step])
            whole = join(mine, other, self.odd_dp == 1, axis)
            at = (self.at_row - step) % self.row
            full = lax.dynamic_update_slice_in_dim(full, whole, at * size, axis)
        return full, mine

    def gather_all(self, block):
        other = flip(block, "col", self.col, 2)
        both = join(block[None], other[None], self.pair == 1, 0)
        mine, last = self.gather_rows(both, 1)
        other = flip(mine, "col", self.col, 1)
        first = jnp.where(self.core == 1, other, mine)
        second = jnp.where(self.core == 1, mine, other)
        return [first[0], second[0], first[1], second[1]], last

    def gather_small(self, block):
        other = flip(block, "col", self.col, 2)
        both = join(block[None], other[None], self.pair == 1, 0)
        other = flip(both, "col", self.col, 1)
        both, other = both[:, None], other[:, None]
        whole = join(both, other, self.core == 1, 1)
        return whole.reshape((self.col,) + block.shape)

    def swap_halves(self, part):
        size = part.shape[0] // self.row
        blocks = part.reshape(self.row, size, part.shape[1])
        mine = half_of(blocks, self.odd_dp, 1)
        return mine, flip(half_of(blocks, 1 - self.odd_dp, 1), "dp", self.dp, 1)

    def scatter_half(self, mine, holds=()):
        def block_at(step):
            at = (self.at_row - step) % self.row
            return lax.dynamic_index_in_dim(mine, at, 0, False).astype(jnp.float32)

        total = low(block_at(1))
        for step in range(1, self.row):
            got = shift(total, "row", self.row)
            if holds:
                got = after(got, holds[step - 1])
            total = low(got.astype(jnp.float32) + block_at(step + 1))
        bit = 2
        while bit < self.dp:
            got = flip(total, "dp", self.dp, bit)
            total = low(total.astype(jnp.float32) + got.astype(jnp.float32))
            bit *= 2
        return total

    def both_halves(self, total):
        other = flip(total, "dp", self.dp, 1)
        return join(total, other, self.odd_dp == 1, 0)

    def scatter_all(self, pieces):
        evens = jnp.stack([pieces[0], pieces[2]])
        odds = jnp.stack([pieces[1], pieces[3]])
        mine = jnp.where(self.core == 1, odds, evens)
        theirs = jnp.where(self.core == 1, evens, odds)
        got = flip(theirs, "col", self.col, 1)
        mine = add(mine, got)
        got = flip(jnp.where(self.pair == 1, mine[0], mine[1]), "col", self.col, 2)
        mine = jnp.where(self.pair == 1, mine[1], mine[0])
        mine, got = self.swap_halves(add(mine, got))
        return self.both_halves(self.scatter_half(add(mine, got)))

    def sum_small(self, values):
        for axis, size in (("col", self.col), ("row", self.row), ("dp", self.dp)):
            bit = 1
            while bit < size:
                values = values + flip(values, axis, size, bit)
                bit *= 2
        return values


def turn_pairs(values, cosine, sine):
    lane = lax.broadcasted_iota(jnp.int32, values.shape, 1)
    before = pltpu.roll(values, HD // 2, 1)
    after = pltpu.roll(values, LANES - HD // 2, 1)
    partner = jnp.where(lane % HD < HD // 2, after, before)
    return values * cosine + partner * sine


def joint_kernel(x_ref, gain_ref, weight_ref, bias_ref, cos_ref, sin_ref, act_ref, out_ref):
    inputs = x_ref[...].astype(jnp.float32)
    inverse = lax.rsqrt(jnp.mean(inputs * inputs, -1, keepdims=True) + EPS)
    act = low(inputs * inverse * gain_ref[...])
    act_ref[...] = act
    joint = dot(act, weight_ref[...]) + bias_ref[...]
    cosine, sine = cos_ref[...], sin_ref[...]
    for start in range(0, QK_WIDTH, LANES):
        turned = turn_pairs(joint[:, start : start + LANES], cosine, sine)
        out_ref[:, start : start + LANES] = low(turned)
    out_ref[:, QK_WIDTH:] = low(joint[:, QK_WIDTH:])


def joint_projection(inputs, gain, weight, bias, cosine, sine):
    tokens, width = inputs.shape
    steps = SEQ_LEN // BLOCK
    return pl.pallas_call(
        joint_kernel,
        grid=(tokens // BLOCK,),
        in_specs=[
            pl.BlockSpec((BLOCK, width), lambda i: (i, 0)),
            pl.BlockSpec((1, width), lambda i: (0, 0)),
            pl.BlockSpec((width, QKV), lambda i: (0, 0)),
            pl.BlockSpec((1, QKV), lambda i: (0, 0)),
            pl.BlockSpec((BLOCK, LANES), lambda i: (i % steps, 0)),
            pl.BlockSpec((BLOCK, LANES), lambda i: (i % steps, 0)),
        ],
        out_specs=[
            pl.BlockSpec((BLOCK, width), lambda i: (i, 0)),
            pl.BlockSpec((BLOCK, QKV), lambda i: (i, 0)),
        ],
        out_shape=[
            jax.ShapeDtypeStruct((tokens, width), jnp.bfloat16),
            jax.ShapeDtypeStruct((tokens, QKV), jnp.bfloat16),
        ],
        compiler_params=pltpu.CompilerParams(vmem_limit_bytes=VMEM_BYTES),
        cost_estimate=cost(2 * tokens * width * QKV * 2, 8 * tokens * QKV),
        name="joint_projection",
    )(inputs, gain, weight, bias, cosine, sine)


def select_head(values, head):
    return jnp.where(head // GROUP == 0, values[:, :HD], values[:, HD:])


def attend_kernel(first, q_ref, k_ref, v_ref, out_ref):
    pair = pl.program_id(1) + first
    scale = HD ** (-0.5)
    for e in range(2):
        keys = select_head(k_ref[...], 2 * pair + e)
        values = select_head(v_ref[...], 2 * pair + e)
        for i in range(SEQ_LEN // BLOCK):
            rows, end = pl.ds(i * BLOCK, BLOCK), (i + 1) * BLOCK
            query = q_ref[rows, e * HD : (e + 1) * HD] * jnp.bfloat16(scale)
            scores = dot(query, keys[:end], NT)
            rows_at = i * BLOCK + lax.broadcasted_iota(jnp.int32, scores.shape, 0)
            keys_at = lax.broadcasted_iota(jnp.int32, scores.shape, 1)
            scores = jnp.where(keys_at <= rows_at, scores, MASKED)
            weights = jnp.exp(scores - jnp.max(scores, -1, keepdims=True))
            total = jnp.sum(weights, -1, keepdims=True)
            attended = dot(low(weights), values[:end]) / total
            out_ref[rows, e * HD : (e + 1) * HD] = low(attended)


def attend(joint, first, pairs):
    tokens = joint.shape[0]
    seqs = tokens // SEQ_LEN
    return pl.pallas_call(
        functools.partial(attend_kernel, first),
        grid=(seqs, pairs),
        in_specs=[
            pl.BlockSpec((SEQ_LEN, LANES), lambda s, p: (s, p + first)),
            pl.BlockSpec((SEQ_LEN, LANES), lambda s, p: (s, WIDTH // LANES)),
            pl.BlockSpec((SEQ_LEN, LANES), lambda s, p: (s, QK_WIDTH // LANES)),
        ],
        out_specs=pl.BlockSpec((SEQ_LEN, LANES), lambda s, p: (s, p)),
        out_shape=jax.ShapeDtypeStruct((tokens, pairs * LANES), jnp.bfloat16),
        compiler_params=pltpu.CompilerParams(vmem_limit_bytes=VMEM_BYTES),
        cost_estimate=cost(
            tokens * SEQ_LEN * pairs * 1024, 8 * tokens * pairs * LANES, tokens * 1024 * pairs
        ),
        name="attend",
    )(joint, joint, joint)


def attend_back_kernel(first, last, *refs):
    if first > 0:
        q_ref, k_ref, v_ref, g_ref, cos_ref, sin_ref, key_in, value_in = refs[:8]
    else:
        q_ref, k_ref, v_ref, g_ref, cos_ref, sin_ref = refs[:6]
    dq_ref, dk_ref, dv_ref, key_sum, value_sum = refs[-5:]
    pair = pl.program_id(1) + first
    scale = HD ** (-0.5)

    @pl.when(pair == first)
    def _():
        key_sum[...] = key_in[...] if first > 0 else jnp.zeros_like(key_sum)
        value_sum[...] = value_in[...] if first > 0 else jnp.zeros_like(value_sum)

    for i in range(SEQ_LEN // BLOCK):
        rows, end = pl.ds(i * BLOCK, BLOCK), (i + 1) * BLOCK
        parts = []
        for e in range(2):
            head = 2 * pair + e
            kv = head // GROUP
            keys = select_head(k_ref[:end, :], head)
            values = select_head(v_ref[:end, :], head)
            query = q_ref[rows, e * HD : (e + 1) * HD] * jnp.bfloat16(scale)
            grad = g_ref[rows, e * HD : (e + 1) * HD]
            scores = dot(keys, query, NT)
            keys_at = lax.broadcasted_iota(jnp.int32, scores.shape, 0)
            rows_at = i * BLOCK + lax.broadcasted_iota(jnp.int32, scores.shape, 1)
            scores = jnp.where(keys_at <= rows_at, scores, MASKED)
            weights = jnp.exp(scores - jnp.max(scores, 0, keepdims=True))
            prob = weights * (1.0 / jnp.sum(weights, 0, keepdims=True))
            prob_grad = dot(values, grad, NT)
            inner = jnp.sum(prob * prob_grad, 0, keepdims=True)
            score_grad = low(prob * (prob_grad - inner))
            value_sum[kv, :end, :] += dot(low(prob), grad)
            key_sum[kv, :end, :] += dot(score_grad, query)
            parts.append(dot(keys, score_grad, TN))
        query_grad = jnp.transpose(jnp.concatenate(parts, 0)) * scale
        turned = turn_pairs(query_grad, cos_ref[rows, :], -sin_ref[rows, :])
        dq_ref[rows, :] = low(turned)

    @pl.when(pair == last)
    def _():
        if last < QH // 2 - 1:
            dk_ref[...] = key_sum[...]
            dv_ref[...] = value_sum[...]
            return
        key_grad = jnp.concatenate([key_sum[0], key_sum[1]], 1)
        dk_ref[...] = low(turn_pairs(key_grad, cos_ref[...], -sin_ref[...]))
        dv_ref[...] = low(jnp.concatenate([value_sum[0], value_sum[1]], 1))


def attend_back(joint, grad, cosine, sine, first, pairs, sums):
    tokens = joint.shape[0]
    last = first + pairs - 1
    ends = last == QH // 2 - 1
    seqs = tokens // SEQ_LEN
    block = (SEQ_LEN, LANES)
    held = pl.BlockSpec((KVH, SEQ_LEN, HD), lambda s, p: (s, 0, 0))
    return pl.pallas_call(
        functools.partial(attend_back_kernel, first, last),
        grid=(seqs, pairs),
        in_specs=[
            pl.BlockSpec(block, lambda s, p: (s, p + first)),
            pl.BlockSpec(block, lambda s, p: (s, WIDTH // LANES)),
            pl.BlockSpec(block, lambda s, p: (s, QK_WIDTH // LANES)),
            pl.BlockSpec(block, lambda s, p: (s, p + first)),
            pl.BlockSpec(block, lambda s, p: (0, 0)),
            pl.BlockSpec(block, lambda s, p: (0, 0)),
        ]
        + ([] if sums is None else [held, held]),
        out_specs=[
            pl.BlockSpec(block, lambda s, p: (s, p)),
        ]
        + [pl.BlockSpec(block, lambda s, p: (s, 0)) if ends else held] * 2,
        out_shape=[
            jax.ShapeDtypeStruct((tokens, pairs * LANES), jnp.bfloat16),
        ]
        + [
            jax.ShapeDtypeStruct((tokens, KV_WIDTH), jnp.bfloat16)
            if ends
            else jax.ShapeDtypeStruct((seqs * KVH, SEQ_LEN, HD), jnp.float32)
        ]
        * 2,
        scratch_shapes=[
            pltpu.VMEM((KVH, SEQ_LEN, HD), jnp.float32),
            pltpu.VMEM((KVH, SEQ_LEN, HD), jnp.float32),
        ],
        compiler_params=pltpu.CompilerParams(vmem_limit_bytes=VMEM_BYTES),
        cost_estimate=cost(
            tokens * SEQ_LEN * pairs * 2560, 8 * tokens * pairs * LANES, tokens * 1024 * pairs
        ),
        name="attend_back",
    )(joint, joint, joint, grad, cosine, sine, *(sums or ()))


def feed_kernel(
    act_ref, cot_ref, weight_ref, mix_ref, grad_ref, hid_ref, dgate_ref, dup_ref
):
    act, cot = act_ref[...], cot_ref[...]
    gate_ref, up_ref, down_ref = weight_ref.at[0], weight_ref.at[1], weight_ref.at[2]
    gate = dot(act, gate_ref[...])
    up_part = dot(act, up_ref[...])
    hidden_grad = dot(cot, down_ref[...])
    sigma = jax.nn.sigmoid(gate)
    silu = gate * sigma
    hidden = low(silu * up_part)
    gate_grad = low(hidden_grad * up_part * sigma * (1.0 + gate * (1.0 - sigma)))
    up_grad = low(hidden_grad * silu)
    hid_ref[...] = hidden
    dgate_ref[...] = gate_grad
    dup_ref[...] = up_grad
    mix_ref[...] = low(dot(hidden, down_ref[...], NT))
    grad_ref[...] = low(dot(gate_grad, gate_ref[...], NT) + dot(up_grad, up_ref[...], NT))


def feed(act, cot, weights):
    tokens, width = act.shape
    inner = weights.shape[2]
    narrow = pl.BlockSpec((BLOCK, width), lambda i: (i, 0))
    wide = pl.BlockSpec((BLOCK, inner), lambda i: (i, 0))
    weight = pl.BlockSpec((3, width, inner), lambda i: (0, 0, 0))
    return pl.pallas_call(
        feed_kernel,
        grid=(tokens // BLOCK,),
        in_specs=[narrow, narrow, weight],
        out_specs=[narrow, narrow, wide, wide, wide],
        out_shape=[jax.ShapeDtypeStruct((tokens, width), jnp.bfloat16)] * 2
        + [jax.ShapeDtypeStruct((tokens, inner), jnp.bfloat16)] * 3,
        compiler_params=pltpu.CompilerParams(vmem_limit_bytes=VMEM_BYTES),
        cost_estimate=cost(
            12 * tokens * width * inner, 2 * tokens * (4 * width + 3 * inner), tokens * inner
        ),
        name="feed",
    )(act, cot, weights)


def normalize_back(values, inverse, gain, upstream):
    weighted = upstream * gain
    inner = jnp.mean(weighted * values, -1, keepdims=True)
    value_grad = inverse * weighted - values * inverse * inverse * inverse * inner
    gain_grad = jnp.sum(upstream * values * inverse, 0)
    return (value_grad, gain_grad)


def inverse_of(values):
    return lax.rsqrt(jnp.mean(values * values, -1, keepdims=True) + EPS)


def rotary_tables():
    freq = BASE ** (-(jnp.arange(HD // 2, dtype=jnp.float32) * 2.0 / HD))
    angle = jnp.arange(SEQ_LEN, dtype=jnp.float32)[:, None] * freq[None, :]
    cosine, sine = jnp.cos(angle), jnp.sin(angle)
    cosine = jnp.concatenate([cosine] * 4, 1)
    sine = jnp.concatenate([-sine, sine, -sine, sine], 1)
    return cosine, sine


def body(
    sizes,
    block_input,
    first_gain,
    joint_weight,
    joint_bias,
    output_weight,
    second_gain,
    gate_weight,
    up_weight,
    down_weight,
    cotangent,
):
    grid = Grid(sizes)
    shard = gate_weight.shape[1]
    inner = -(-shard // LANES) * LANES
    wide = ((0, 0), (0, inner - shard))
    gain_size, bias_size = first_gain.shape[0], joint_bias.shape[0]
    stretch = (0, bias_size - gain_size)
    small = jnp.stack([joint_bias, jnp.pad(first_gain, stretch), jnp.pad(second_gain, stretch)])
    small = grid.gather_small(small)
    bias_full = small[:, 0].reshape(1, -1).astype(jnp.float32)
    first_scale = small[:, 1, :gain_size].reshape(1, -1).astype(jnp.float32)
    second_scale = small[:, 2, :gain_size].reshape(1, -1).astype(jnp.float32)
    columns = jnp.concatenate([joint_weight, output_weight], 1)
    blocks, last = grid.gather_all(columns)
    joint_full = jnp.concatenate([block[:, :bias_size] for block in blocks], 1)
    output_full = jnp.concatenate([block[:, bias_size:] for block in blocks], 1)
    cosine, sine = rotary_tables()
    size = sizes["col"]
    cot_near = flip(cotangent, "col", size, 1)
    cot_far = flip(cotangent, "col", size, 2)

    first_act, joint = joint_projection(
        block_input, first_scale, joint_full, bias_full, cosine, sine
    )
    attended_low = attend(joint, 0, 4)
    attended_high = attend(joint, 4, 3)
    attended = jnp.concatenate([attended_low, attended_high], 1)
    inputs = block_input.astype(jnp.float32)
    resid = inputs + dot(attended, output_full)
    second_inverse = inverse_of(resid)
    second_act = low(resid * second_inverse * second_scale)
    weights = jnp.stack([gate_weight, up_weight, down_weight.T])
    weights = after(jnp.pad(weights, ((0, 0),) + wide), last)
    holds = (joint, attended_low, attended_high, second_act)
    weights, _ = grid.gather_rows(weights, 1, holds)

    act_near = flip(second_act, "col", size, 1)
    act_far = flip(second_act, "col", size, 2)
    cot_last = flip(after(cot_far, joint), "col", size, 1)
    fed_own = feed(second_act, cotangent, weights)
    fed_near = feed(act_near, cot_near, weights)
    act_far = after(act_far, fed_near[0])
    act_last = flip(act_far, "col", size, 1)
    fed_far = feed(act_far, cot_far, weights)
    fed_last = feed(act_last, cot_last, weights)
    fed = (fed_own, fed_near, fed_far, fed_last)

    got_near = flip(fed_near[1], "col", size, 1)
    got_last = flip(fed_last[1], "col", size, 1)
    got_far = flip(add(fed_far[1], got_last), "col", size, 2)

    act_all = jnp.concatenate([second_act, act_near, act_far, act_last], 0)
    cot_all = jnp.concatenate([cotangent, cot_near, cot_far, cot_last], 0)
    hidden, gate_grad, up_grad = (
        jnp.concatenate([item[at] for item in fed], 0) for at in (2, 3, 4)
    )
    down_part = low(dot(cot_all, hidden, TN))
    down_mine, down_got = grid.swap_halves(down_part)
    gate_part = low(dot(act_all, after(gate_grad, down_part), TN))
    gate_mine, gate_got = grid.swap_halves(gate_part)
    up_part = low(dot(act_all, after(up_grad, gate_part), TN))
    up_mine, up_got = grid.swap_halves(up_part)

    got_far = after(got_far, up_part)
    second_grad = fed_own[1].astype(jnp.float32) + got_near.astype(jnp.float32)
    second_grad = second_grad + got_far.astype(jnp.float32)
    resid_norm_grad, second_gain_grad = normalize_back(
        resid, second_inverse, second_scale, second_grad
    )
    resid_grad = cotangent.astype(jnp.float32) + resid_norm_grad
    proj_grad = low(resid_grad)
    attended_grad = low(dot(proj_grad, output_full, NT))

    mix_last = flip(after(fed_last[0], got_far), "col", size, 1)
    mix_near = flip(after(fed_near[0], got_far), "col", size, 1)

    back = attend_back(joint, attended_grad, cosine, sine, 0, 3, None)
    query_low, sums = back[0], back[1:]
    mix_far = flip(add(fed_far[0], after(mix_last, attended_grad)), "col", size, 2)
    down_mine = add(down_mine, after(down_got, up_part))
    down_total = grid.scatter_half(down_mine, (attended_grad, query_low, query_low))
    query_mid, *sums = attend_back(joint, attended_grad, cosine, sine, 3, 2, sums)
    gate_mine = add(gate_mine, after(gate_got, query_low))
    up_mine = add(up_mine, after(up_got, query_mid))
    query_high, key_grad, value_grad = attend_back(
        joint, attended_grad, cosine, sine, 5, 2, sums
    )
    both = jnp.concatenate([gate_mine, up_mine], 1)
    both_total = grid.scatter_half(both, (query_high, query_high, query_high))
    down_w_grad = grid.both_halves(after(down_total, query_mid))

    joint_grad = jnp.concatenate([query_low, query_mid, query_high, key_grad, value_grad], 1)
    joint_part = low(dot(first_act, joint_grad, TN))
    output_part = low(dot(attended, proj_grad, TN))
    pieces = [
        jnp.concatenate(
            [
                joint_part[:, j * bias_size : (j + 1) * bias_size],
                output_part[:, j * gain_size : (j + 1) * gain_size],
            ],
            1,
        )
        for j in range(size)
    ]
    block_grad = grid.scatter_all(pieces)
    joint_w_grad, output_w_grad = block_grad[:, :bias_size], block_grad[:, bias_size:]
    bias_grad = jnp.sum(joint_grad.astype(jnp.float32), 0)
    first_grad = dot(joint_grad, joint_full, NT)
    first_inverse = inverse_of(inputs)
    input_norm_grad, first_gain_grad = normalize_back(
        inputs, first_inverse, first_scale, first_grad
    )
    input_grad = low(resid_grad + input_norm_grad)
    totals = grid.sum_small(jnp.concatenate([bias_grad, first_gain_grad, second_gain_grad]))

    mix_far = after(mix_far, query_high).astype(jnp.float32)
    mixed = fed_own[0].astype(jnp.float32) + mix_near.astype(jnp.float32) + mix_far
    block_output = low(resid + mixed)
    half = both_total.shape[0] // 2
    other = flip(both_total, "dp", sizes["dp"], 1)
    gate_w_grad, up_w_grad = (
        join(both_total[at : at + half], other[at : at + half], grid.odd_dp == 1, 0)
        for at in (0, half)
    )

    def own(start, size):
        part = size // grid.col
        return lax.dynamic_slice_in_dim(totals, start + grid.at_col * part, part, 0)

    model = first_gain_grad.shape[0]
    wide_out = lambda values: values.astype(jnp.float32)
    return (
        block_output,
        input_grad,
        own(QKV, model),
        wide_out(joint_w_grad),
        own(0, QK_WIDTH),
        own(QK_WIDTH, KV_WIDTH),
        wide_out(output_w_grad),
        own(QKV + model, model),
        wide_out(gate_w_grad[:, :shard]),
        wide_out(up_w_grad[:, :shard]),
        wide_out(down_w_grad[:, :shard].T),
    )


def solution(mesh):
    tokens = P(("dp", "row", "col"), None)
    return jax.shard_map(
        functools.partial(body, dict(mesh.shape)),
        mesh=mesh,
        in_specs=(
            tokens,
            P("col"),
            P("row", "col"),
            P("col"),
            P("row", "col"),
            P("col"),
            P("row", "col"),
            P("row", "col"),
            P("col", "row"),
            tokens,
        ),
        out_specs=(
            tokens,
            tokens,
            P("col"),
            P("row", "col"),
            P("col"),
            P("col"),
            P("row", "col"),
            P("col"),
            P("row", "col"),
            P("row", "col"),
            P("col", "row"),
        ),
        check_vma=False,
    )
```

time: 1240 us -> 599 us (0.48)
  waiting for transfers between devices: 524 us -> 191 us
  matrix products: 385 us -> 62.6 us
  Pallas kernels: 0 us -> 185 us
  blocking collectives: 77.5 us -> 0 us
  local copies, waits for them, and re-layouts: 110 us -> 41.7 us
  starting transfers between devices: 0.99 us -> 33.6 us
  loops' own time: 27.1 us -> 0 us
  between operations: 18.3 us -> 2.34 us
    dot_general x43 -> x8, matrix products: 385 us -> 62.6 us  [dot(): lax.dot_general(left, right, dims, preferred_element_type=jnp.float32)]
    reduce_scatter x5 -> x0, waiting for transfers between devices: 199 us -> none  [the longest x1 72 us: body(): lax.psum_scatter(gate_w_grad.astype(jnp.bfloat16), 'col', scatter_dimensi...]
    ppermute x0 -> x51, waiting for transfers between devices: none -> 191 us  [the longest x36 114 us: flip(): return lax.ppermute(values, axis, [(i, i ^ bit) for i in range(size)])]
    pallas_call x0 -> x10, Pallas kernels: none -> 185 us  [the longest x4 91.2 us: feed(): pl.pallas_call(feed_kernel, grid=(tokens // BLOCK,), in_specs=[narrow, na...]
    unnamed x24 -> x0, waiting for transfers between devices: 168 us -> none
    all_gather x8 -> x0, waiting for transfers between devices: 138 us -> none  [the longest x1 45.8 us: body(): lax.all_gather(up_weight, 'row', axis=0, tiled=True)]
    unnamed x83 -> x124, local copies, waits for them, and re-layouts: 56.6 us -> 12 us
    all_gather x2 -> x0, blocking collectives: 42.4 us -> none  [the longest x1 21.8 us: body(): lax.all_gather(joint_weight, 'row', axis=0, tiled=True)]
  transfers between devices with their start and end apart: 19 -> 51, of which waited for: 14 -> 21; matrix products, arithmetic and copies ran while one was open for 39% -> 28% of each run, Pallas kernels for 0% -> 31%
where the time goes in v1:
time: 599 us; the launch traced here: 592 us
  waiting for transfers between devices  191 us (32%)
  Pallas kernels  185 us (31%)
  other arithmetic  75.7 us (13%)
  matrix products  62.6 us (10%)
  local copies, waits for them, and re-layouts  41.7 us (7%)
  starting transfers between devices  33.6 us (6%)
    ppermute x36, waiting for transfers between devices, flip(): return lax.ppermute(values, axis, [(i, i ^ bit) for i in range(size)])  114 us
    pallas_call x4, Pallas kernels, feed(): pl.pallas_call(feed_kernel, grid=(tokens // BLOCK,), in_specs=[narrow, na...  91.2 us
    ppermute x15, waiting for transfers between devices, shift(): lax.ppermute(values, axis, [(i, (i + 1) % size) for i in range(size)])  77.1 us
    dot_general x8, matrix products, dot(): lax.dot_general(left, right, dims, preferred_element_type=jnp.float32)  62.6 us
    pallas_call x3, Pallas kernels, attend_back(): pl.pallas_call(functools.partial(attend_back_kernel, first, last), grid=(...  57.3 us
    pallas_call x2, Pallas kernels, attend(): pl.pallas_call(functools.partial(attend_kernel, first), grid=(seqs, pairs...  29.1 us
    ppermute x36, starting transfers between devices, flip(): return lax.ppermute(values, axis, [(i, i ^ bit) for i in range(size)])  28.7 us
    convert_element_type x20, other arithmetic, low(): return values.astype(jnp.bfloat16)  22.6 us
  transfers between devices with their start and end apart: 51, of which 21 were waited for; matrix products, arithmetic and copies ran while one was open for 28% of the time, Pallas kernels for 31%

profile of v1, /device:TPU:0, one launch (start us, length us, event | category | flops | bytes accessed | tf_op | source)
XLA Modules:
  0.0 591.5 jit_solution(9275054070175406284)
XLA Ops:
  12.9 36.1 %collective-permute-done.2 = bf16[224,512]{1,0:T(8,128)(2,1)} collective-permute-done((bf16[224,512]{1,0:T(8,128)(2,1)}, bf16[224,512]{1,0:T(8,128)(2,1)}, u32[]{:S(2)}, u32[]{:S(2)}) %collective-permute-start.2) | collective-permute-done | bytes 229408 | tf_op jit(solution)/shard_map/ppermute | solution.py:51
  63.0 4.9 collective-permute-done.5
  70.5 5.4 collective-permute-done.7
  106.3 4.0 concatenate.100.weight_ref
  110.3 7.4 %joint_projection.1 = (bf16[1024,896]{1,0:T(8,128)(2,1)}, bf16[1024,1152]{1,0:T(8,128)(2,1)}) custom-call(bf16[1024,896]{1,0:T(8,128)(2,1)} %x_ref.1, f32[1,896]{1,0:T(1,128)} %reshape.142.gain_ref, bf16[896,1152]{1,0:T(8,128)(2,1)} %concatenate.100.weight_ref, f32[1,1152]{1,0:T(1,128)} %reshape.143.bias_ref, ...), custom_call_target="tpu_custom_call" | custom-call | flops 4227858432 | bytes 9437184 | tf_op jit(solution)/shard_map/joint_projection/pallas_call | solution.py:192
  117.7 4.4 collective-permute-done.10
  123.7 12.7 %attend.3 = bf16[1024,384]{1,0:T(8,128)(2,1)} custom-call(bf16[1024,1152]{1,0:T(8,128)(2,1)} %get-tuple-element.68.q_ref.k_ref.v_ref.refs_0_.refs_1_.refs_2_, bf16[1024,1152]{1,0:T(8,128)(2,1)} %get-tuple-element.68.q_ref.k_ref.v_ref.refs_0_.refs_1_.refs_2_, bf16[1024,1152]{1,0:T(8,128)(2,1)} %get-tuple-element.68.q_ref.k_ref.v_ref.refs_0_.refs_1_.refs_2_), custom_call_target="tpu_custom_call" | custom-call | flops 3221225472 | bytes 3145728 | tf_op jit(solution)/shard_map/attend/pallas_call | solution.py:243
  136.5 16.4 %attend.2 = bf16[1024,512]{1,0:T(8,128)(2,1)} custom-call(bf16[1024,1152]{1,0:T(8,128)(2,1)} %get-tuple-element.68.q_ref.k_ref.v_ref.refs_0_.refs_1_.refs_2_, bf16[1024,1152]{1,0:T(8,128)(2,1)} %get-tuple-element.68.q_ref.k_ref.v_ref.refs_0_.refs_1_.refs_2_, bf16[1024,1152]{1,0:T(8,128)(2,1)} %get-tuple-element.68.q_ref.k_ref.v_ref.refs_0_.refs_1_.refs_2_), custom_call_target="tpu_custom_call" | custom-call | flops 4294967296 | bytes 4194304 | tf_op jit(solution)/shard_map/attend/pallas_call | solution.py:243
  163.7 20.2 %collective-permute-done.14 = bf16[3,112,1280]{2,1,0:T(8,128)(2,1)S(1)} collective-permute-done((bf16[3,112,1280]{2,1,0:T(8,128)(2,1)S(1)}, bf16[3,112,1280]{2,1,0:T(8,128)(2,1)S(1)}, u32[]{:S(2)}, u32[]{:S(2)}) %collective-permute-start.14) | collective-permute-done | bytes 860192 | tf_op jit(solution)/shard_map/ppermute | solution.py:55
  185.9 19.5 %collective-permute-done.15 = bf16[3,112,1280]{2,1,0:T(8,128)(2,1)S(1)} collective-permute-done((bf16[3,112,1280]{2,1,0:T(8,128)(2,1)S(1)}, bf16[3,112,1280]{2,1,0:T(8,128)(2,1)S(1)}, u32[]{:S(2)}, u32[]{:S(2)}) %collective-permute-start.15) | collective-permute-done | bytes 860192 | tf_op jit(solution)/shard_map/ppermute | solution.py:51
  208.1 22.6 %feed.5 = (bf16[1024,896]{1,0:T(8,128)(2,1)}, bf16[1024,896]{1,0:T(8,128)(2,1)}, bf16[1024,1280]{1,0:T(8,128)(2,1)}, bf16[1024,1280]{1,0:T(8,128)(2,1)}, bf16[1024,1280]{1,0:T(8,128)(2,1)}) custom-call(bf16[1024,896]{1,0:T(8,128)(2,1)} %copy-done.53, bf16[1024,896]{1,0:T(8,128)(2,1)} %collective-permute-done.17.cot_ref, ...), custom_call_target="tpu_custom_call" | custom-call | flops 14092861440 | bytes 15204352 | tf_op jit(solution)/shard_map/feed/pallas_call | solution.py:382
  230.8 23.2 %feed.4 = (bf16[1024,896]{1,0:T(8,128)(2,1)}, bf16[1024,896]{1,0:T(8,128)(2,1)}, bf16[1024,1280]{1,0:T(8,128)(2,1)}, bf16[1024,1280]{1,0:T(8,128)(2,1)}, bf16[1024,1280]{1,0:T(8,128)(2,1)}) custom-call(bf16[1024,896]{1,0:T(8,128)(2,1)} %copy-done.23, bf16[1024,896]{1,0:T(8,128)(2,1)} %cot_ref.1, ...), custom_call_target="tpu_custom_call" | custom-call | flops 14092861440 | bytes 15204352 | tf_op jit(solution)/shard_map/feed/pallas_call | solution.py:382
  254.1 22.6 %feed.6 = (bf16[1024,896]{1,0:T(8,128)(2,1)}, bf16[1024,896]{1,0:T(8,128)(2,1)}, bf16[1024,1280]{1,0:T(8,128)(2,1)}, bf16[1024,1280]{1,0:T(8,128)(2,1)}, bf16[1024,1280]{1,0:T(8,128)(2,1)}) custom-call(bf16[1024,896]{1,0:T(8,128)(2,1)} %copy-done.52, bf16[1024,896]{1,0:T(8,128)(2,1)} %collective-permute-done.19.cot_ref, ...), custom_call_target="tpu_custom_call" | custom-call | flops 14092861440 | bytes 15204352 | tf_op jit(solution)/shard_map/feed/pallas_call | solution.py:382
  277.9 22.8 %feed.7 = (bf16[1024,896]{1,0:T(8,128)(2,1)}, bf16[1024,896]{1,0:T(8,128)(2,1)}, bf16[1024,1280]{1,0:T(8,128)(2,1)}, bf16[1024,1280]{1,0:T(8,128)(2,1)}, bf16[1024,1280]{1,0:T(8,128)(2,1)}) custom-call(bf16[1024,896]{1,0:T(8,128)(2,1)} %copy-done.54, bf16[1024,896]{1,0:T(8,128)(2,1)} %collective-permute-done.21.cot_ref, ...), custom_call_target="tpu_custom_call" | custom-call | flops 14092861440 | bytes 15204352 | tf_op jit(solution)/shard_map/feed/pallas_call | solution.py:382
  301.2 17.6 %fusion.25 = bf16[896,1280]{1,0:T(8,128)(2,1)} fusion(bf16[1024,1280]{1,0:T(8,128)(2,1)} %get-tuple-element.93, bf16[1024,1280]{1,0:T(8,128)(2,1)} %get-tuple-element.92, bf16[1024,1280]{1,0:T(8,128)(2,1)} %get-tuple-element.91, bf16[1024,1280]{1,0:T(8,128)(2,1)} %get-tuple-element.90, bf16[1024,896]{1,0:T(8,128)(2,1)} %collective-permute-done.21.cot_ref, ...), kind=kOutput, calls=%fused_computation.44 | convolution fusion | flops 9467691008 | bytes 20119552 | tf_op jit(solution)/shard_map/dot_general | solution.py:33
  321.7 5.3 pad_maximum_fusion.1
  327.0 15.0 %convolution_convert_fusion.2 = bf16[896,1280]{1,0:T(8,128)(2,1)} fusion(bf16[4096,1280]{1,0:T(8,128)(2,1)S(1)} %pad_maximum_fusion.1, bf16[1024,896]{1,0:T(8,128)(2,1)} %copy-done.54, bf16[1024,896]{1,0:T(8,128)(2,1)} %copy-done.52, bf16[1024,896]{1,0:T(8,128)(2,1)} %copy-done.53, bf16[1024,896]{1,0:T(8,128)(2,1)} %copy-done.23), kind=kOutput, calls=%fused_computation.47 | convolution fusion | flops 9425747968 | bytes 20119552 | tf_op jit(solution)/shard_map/dot_general | solution.py:33
  342.0 5.5 pad_maximum_fusion
  353.9 14.7 %convolution_convert_fusion.1 = bf16[896,1280]{1,0:T(8,128)(2,1)} fusion(bf16[4096,1280]{1,0:T(8,128)(2,1)S(1)} %pad_maximum_fusion, bf16[1024,896]{1,0:T(8,128)(2,1)} %copy-done.54, bf16[1024,896]{1,0:T(8,128)(2,1)} %copy-done.52, bf16[1024,896]{1,0:T(8,128)(2,1)} %copy-done.53, bf16[1024,896]{1,0:T(8,128)(2,1)} %copy-done.23), kind=kOutput, calls=%fused_computation.46 | convolution fusion | flops 9425747968 | bytes 20119552 | tf_op jit(solution)/shard_map/dot_general | solution.py:33
  373.4 21.6 %collective-permute-done.23 = bf16[1024,896]{1,0:T(8,128)(2,1)} collective-permute-done((bf16[1024,896]{1,0:T(8,128)(2,1)}, bf16[1024,896]{1,0:T(8,128)(2,1)}, u32[]{:S(2)}, u32[]{:S(2)}) %collective-permute-start.23) | collective-permute-done | bytes 1835040 | tf_op jit(solution)/shard_map/ppermute | solution.py:51
  395.1 3.9 multiply_reduce_fusion
  410.0 23.1 %attend_back.3 = (bf16[1024,384]{1,0:T(8,128)(2,1)}, f32[2,1024,64]{2,1,0:T(8,128)}, f32[2,1024,64]{2,1,0:T(8,128)}) custom-call(bf16[1024,1152]{1,0:T(8,128)(2,1)} %get-tuple-element.68.q_ref.k_ref.v_ref.refs_0_.refs_1_.refs_2_, bf16[1024,1152]{1,0:T(8,128)(2,1)} %get-tuple-element.68.q_ref.k_ref.v_ref.refs_0_.refs_1_.refs_2_, ...), custom_call_target="tpu_custom_call" | custom-call | flops 8053063680 | bytes 3145728 | tf_op jit(solution)/shard_map/attend_back/pallas_call | solution.py:319
  434.3 17.0 %attend_back.4 = (bf16[1024,256]{1,0:T(8,128)(2,1)}, f32[2,1024,64]{2,1,0:T(8,128)}, f32[2,1024,64]{2,1,0:T(8,128)}) custom-call(bf16[1024,1152]{1,0:T(8,128)(2,1)} %get-tuple-element.68.q_ref.k_ref.v_ref.refs_0_.refs_1_.refs_2_, bf16[1024,1152]{1,0:T(8,128)(2,1)} %get-tuple-element.68.q_ref.k_ref.v_ref.refs_0_.refs_1_.refs_2_, ...), custom_call_target="tpu_custom_call" | custom-call | flops 5368709120 | bytes 2097152 | tf_op jit(solution)/shard_map/attend_back/pallas_call | solution.py:319
  456.5 17.1 %attend_back.5 = (bf16[1024,256]{1,0:T(8,128)(2,1)}, bf16[1024,128]{1,0:T(8,128)(2,1)}, bf16[1024,128]{1,0:T(8,128)(2,1)}) custom-call(bf16[1024,1152]{1,0:T(8,128)(2,1)} %get-tuple-element.68.q_ref.k_ref.v_ref.refs_0_.refs_1_.refs_2_, bf16[1024,1152]{1,0:T(8,128)(2,1)} %get-tuple-element.68.q_ref.k_ref.v_ref.refs_0_.refs_1_.refs_2_, ...), custom_call_target="tpu_custom_call" | custom-call | flops 5368709120 | bytes 2097152 | tf_op jit(solution)/shard_map/attend_back/pallas_call | solution.py:319
  495.6 6.6 %collective-permute-done.31 = f32[2944]{0:T(1024)S(1)} collective-permute-done((f32[2944]{0:T(1024)S(1)}, f32[2944]{0:T(1024)S(1)}, u32[]{:S(2)}, u32[]{:S(2)}) %collective-permute-start.31) | collective-permute-done | bytes 11808 | tf_op jit(solution)/shard_map/ppermute | solution.py:51
  508.8 13.4 %collective-permute-done.43 = bf16[224,1280]{1,0:T(8,128)(2,1)S(1)} collective-permute-done((bf16[224,1280]{1,0:T(8,128)(2,1)S(1)}, bf16[224,1280]{1,0:T(8,128)(2,1)S(1)}, u32[]{:S(2)}, u32[]{:S(2)}) %collective-permute-start.43) | collective-permute-done | bytes 573472 | tf_op jit(solution)/shard_map/ppermute | solution.py:55
  529.4 10.0 %collective-permute-done.44 = bf16[224,1280]{1,0:T(8,128)(2,1)S(1)} collective-permute-done((bf16[224,1280]{1,0:T(8,128)(2,1)S(1)}, bf16[224,1280]{1,0:T(8,128)(2,1)S(1)}, u32[]{:S(2)}, u32[]{:S(2)}) %collective-permute-start.44) | collective-permute-done | bytes 573472 | tf_op jit(solution)/shard_map/ppermute | solution.py:55
  548.0 9.0 %collective-permute-done.35 = bf16[4,112,512]{2,1,0:T(8,128)(2,1)S(1)} collective-permute-done((bf16[4,112,512]{2,1,0:T(8,128)(2,1)S(1)}, bf16[4,112,512]{2,1,0:T(8,128)(2,1)S(1)}, u32[]{:S(2)}, u32[]{:S(2)}) %collective-permute-start.35) | collective-permute-done | bytes 458784 | tf_op jit(solution)/shard_map/ppermute | solution.py:51
  557.2 7.7 %collective-permute-done.45 = bf16[224,1280]{1,0:T(8,128)(2,1)S(1)} collective-permute-done((bf16[224,1280]{1,0:T(8,128)(2,1)S(1)}, bf16[224,1280]{1,0:T(8,128)(2,1)S(1)}, u32[]{:S(2)}, u32[]{:S(2)}) %collective-permute-start.45) | collective-permute-done | bytes 573472 | tf_op jit(solution)/shard_map/ppermute | solution.py:51
  566.2 6.4 %collective-permute-done.37 = bf16[112,512]{1,0:T(8,128)(2,1)S(1)} collective-permute-done((bf16[112,512]{1,0:T(8,128)(2,1)S(1)}, bf16[112,512]{1,0:T(8,128)(2,1)S(1)}, u32[]{:S(2)}, u32[]{:S(2)}) %collective-permute-start.37) | collective-permute-done | bytes 114720 | tf_op jit(solution)/shard_map/ppermute | solution.py:55
  573.8 5.5 collective-permute-done.38
  585.9 5.1 add_convert_fusion.1
  (327 shorter events, 162.5 us)
Async XLA Ops:
  0.6 159.3 %collective-permute-start.19 = (bf16[1024,896]{1,0:T(8,128)(2,1)}, bf16[1024,896]{1,0:T(8,128)(2,1)}, u32[]{:S(2)}, u32[]{:S(2)}) collective-permute-start(bf16[1024,896]{1,0:T(8,128)(2,1)} %cot_ref.1), channel_id=1, source_target_pairs={{0,2},{1,3},{2,0},{3,1},{4,6},{5,7},{6,4},{7,5},{8,10},{9,11},{10,... | collective-permute-start | bytes 5505032 | tf_op jit(solution)/shard_map/ppermute | solution.py:51
  3.7 203.1 %collective-permute-start.17 = (bf16[1024,896]{1,0:T(8,128)(2,1)}, bf16[1024,896]{1,0:T(8,128)(2,1)}, u32[]{:S(2)}, u32[]{:S(2)}) collective-permute-start(bf16[1024,896]{1,0:T(8,128)(2,1)} %cot_ref.1), channel_id=1, source_target_pairs={{0,1},{1,0},{2,3},{3,2},{4,5},{5,4},{6,7},{7,6},{8,9},{9,8},{10,11... | collective-permute-start | bytes 5505032 | tf_op jit(solution)/shard_map/ppermute | solution.py:51
  6.3 77.0 %collective-permute-start = (bf16[3,288]{1,0:T(4,128)(2,1)}, bf16[3,288]{1,0:T(4,128)(2,1)}, u32[]{:S(2)}, u32[]{:S(2)}) collective-permute-start(bf16[3,288]{1,0:T(4,128)(2,1)} %pad_maximum_fusion.24), channel_id=1, source_target_pairs={{0,2},{1,3},{2,0},{3,1},{4,6},{5,7},{6,4},{7,5},{8,10},{9,11},{10,... | collective-permute-start | bytes 5192 | tf_op jit(solution)/shard_map/ppermute | solution.py:51
  9.3 39.7 %collective-permute-start.2 = (bf16[224,512]{1,0:T(8,128)(2,1)}, bf16[224,512]{1,0:T(8,128)(2,1)}, u32[]{:S(2)}, u32[]{:S(2)}) collective-permute-start(bf16[224,512]{1,0:T(8,128)(2,1)} %pad_maximum_fusion.17), channel_id=1, source_target_pairs={{0,2},{1,3},{2,0},{3,1},{4,6},{5,7},{6,4},{7,5},{8,10},{9,11},{10,... | collective-permute-start | bytes 688136 | tf_op jit(solution)/shard_map/ppermute | solution.py:51
  82.0 17.4 %collective-permute-start.9 = (bf16[2,896,512]{2,1,0:T(8,128)(2,1)S(1)}, bf16[2,896,512]{2,1,0:T(8,128)(2,1)}, u32[]{:S(2)}, u32[]{:S(2)}) collective-permute-start(bf16[2,896,512]{2,1,0:T(8,128)(2,1)S(1)} %maximum_dynamic-update-slice_fusion.5), channel_id=1, source_target_pairs={{0,1},{1,0},{2,3},{3,2},{4,5},{5,4},{6,7},{7,6},{8,9},{9,8},{10,11... | collective-permute-start | bytes 5505032 | tf_op jit(solution)/shard_map/ppermute | solution.py:51
  98.7 23.3 %collective-permute-start.10 = (bf16[3,112,1280]{2,1,0:T(8,128)(2,1)}, bf16[3,112,1280]{2,1,0:T(8,128)(2,1)}, u32[]{:S(2)}, u32[]{:S(2)}) collective-permute-start(bf16[3,112,1280]{2,1,0:T(8,128)(2,1)} %constant_dynamic-slice_fusion.4), channel_id=1, source_target_pairs={{0,4},{4,8},{8,12},{12,0},{1,5},{5,9},{9,13},{13,1},{2,6},{6,10},{... | collective-permute-start | bytes 2580488 | tf_op jit(solution)/shard_map/ppermute | solution.py:55
  122.0 38.0 %collective-permute-start.12 = (bf16[3,112,1280]{2,1,0:T(8,128)(2,1)}, bf16[3,112,1280]{2,1,0:T(8,128)(2,1)S(1)}, u32[]{:S(2)}, u32[]{:S(2)}) collective-permute-start(bf16[3,112,1280]{2,1,0:T(8,128)(2,1)} %collective-permute-done.10), channel_id=1, source_target_pairs={{0,4},{4,8},{8,12},{12,0},{1,5},{5,9},{9,13},{13,1},{2,6},{6,10},{... | collective-permute-start | bytes 2580488 | tf_op jit(solution)/shard_map/ppermute | solution.py:55
  122.2 38.2 %collective-permute-start.11 = (bf16[3,112,1280]{2,1,0:T(8,128)(2,1)}, bf16[3,112,1280]{2,1,0:T(8,128)(2,1)S(1)}, u32[]{:S(2)}, u32[]{:S(2)}) collective-permute-start(bf16[3,112,1280]{2,1,0:T(8,128)(2,1)} %collective-permute-done.10), channel_id=1, source_target_pairs={{0,16},{16,0},{1,17},{17,1},{2,18},{18,2},{3,19},{19,3},{4,20},{20... | collective-permute-start | bytes 2580488 | tf_op jit(solution)/shard_map/ppermute | solution.py:51
  158.5 72.2 %collective-permute-start.18 = (bf16[1024,896]{1,0:T(8,128)(2,1)S(1)}, bf16[1024,896]{1,0:T(8,128)(2,1)S(1)}, u32[]{:S(2)}, u32[]{:S(2)}) collective-permute-start(bf16[1024,896]{1,0:T(8,128)(2,1)S(1)} %multiply_convert_fusion.act_ref), channel_id=1, source_target_pairs={{0,2},{1,3},{2,0},{3,1},{4,6},{5,7},{6,4},{7,5},{8,10},{9,11},{10,... | collective-permute-start | bytes 5505032 | tf_op jit(solution)/shard_map/ppermute | solution.py:51
  160.0 46.8 %collective-permute-start.16 = (bf16[1024,896]{1,0:T(8,128)(2,1)S(1)}, bf16[1024,896]{1,0:T(8,128)(2,1)S(1)}, u32[]{:S(2)}, u32[]{:S(2)}) collective-permute-start(bf16[1024,896]{1,0:T(8,128)(2,1)S(1)} %multiply_convert_fusion.act_ref), channel_id=1, source_target_pairs={{0,1},{1,0},{2,3},{3,2},{4,5},{5,4},{6,7},{7,6},{8,9},{9,8},{10,11... | collective-permute-start | bytes 5505032 | tf_op jit(solution)/shard_map/ppermute | solution.py:51
  160.0 23.9 %collective-permute-start.14 = (bf16[3,112,1280]{2,1,0:T(8,128)(2,1)S(1)}, bf16[3,112,1280]{2,1,0:T(8,128)(2,1)S(1)}, u32[]{:S(2)}, u32[]{:S(2)}) collective-permute-start(bf16[3,112,1280]{2,1,0:T(8,128)(2,1)S(1)} %collective-permute-done.12), channel_id=1, source_target_pairs={{0,4},{4,8},{8,12},{12,0},{1,5},{5,9},{9,13},{13,1},{2,6},{6,10},{... | collective-permute-start | bytes 2580488 | tf_op jit(solution)/shard_map/ppermute | solution.py:55
  160.5 23.4 %collective-permute-start.13 = (bf16[3,112,1280]{2,1,0:T(8,128)(2,1)S(1)}, bf16[3,112,1280]{2,1,0:T(8,128)(2,1)S(1)}, u32[]{:S(2)}, u32[]{:S(2)}) collective-permute-start(bf16[3,112,1280]{2,1,0:T(8,128)(2,1)S(1)} %collective-permute-done.12), channel_id=1, source_target_pairs={{0,16},{16,0},{1,17},{17,1},{2,18},{18,2},{3,19},{19,3},{4,20},{20... | collective-permute-start | bytes 2580488 | tf_op jit(solution)/shard_map/ppermute | solution.py:51
  183.9 92.8 %collective-permute-start.21 = (bf16[1024,896]{1,0:T(8,128)(2,1)}, bf16[1024,896]{1,0:T(8,128)(2,1)}, u32[]{:S(2)}, u32[]{:S(2)}) collective-permute-start(bf16[1024,896]{1,0:T(8,128)(2,1)} %collective-permute-done.19.cot_ref), channel_id=1, source_target_pairs={{0,1},{1,0},{2,3},{3,2},{4,5},{5,4},{6,7},{7,6},{8,9},{9,8},{10,11... | collective-permute-start | bytes 5505032 | tf_op jit(solution)/shard_map/ppermute | solution.py:51
  183.9 21.5 %collective-permute-start.15 = (bf16[3,112,1280]{2,1,0:T(8,128)(2,1)S(1)}, bf16[3,112,1280]{2,1,0:T(8,128)(2,1)S(1)}, u32[]{:S(2)}, u32[]{:S(2)}) collective-permute-start(bf16[3,112,1280]{2,1,0:T(8,128)(2,1)S(1)} %collective-permute-done.14), channel_id=1, source_target_pairs={{0,16},{16,0},{1,17},{17,1},{2,18},{18,2},{3,19},{19,3},{4,20},{20... | collective-permute-start | bytes 2580488 | tf_op jit(solution)/shard_map/ppermute | solution.py:51
  230.7 45.9 %collective-permute-start.20 = (bf16[1024,896]{1,0:T(8,128)(2,1)S(1)}, bf16[1024,896]{1,0:T(8,128)(2,1)S(1)}, u32[]{:S(2)}, u32[]{:S(2)}) collective-permute-start(bf16[1024,896]{1,0:T(8,128)(2,1)S(1)} %collective-permute-done.18.act_ref), channel_id=1, source_target_pairs={{0,1},{1,0},{2,3},{3,2},{4,5},{5,4},{6,7},{7,6},{8,9},{9,8},{10,11... | collective-permute-start | bytes 5505032 | tf_op jit(solution)/shard_map/ppermute | solution.py:51
  254.0 141.1 %collective-permute-start.26 = (bf16[1024,896]{1,0:T(8,128)(2,1)}, bf16[1024,896]{1,0:T(8,128)(2,1)S(1)}, u32[]{:S(2)}, u32[]{:S(2)}) collective-permute-start(bf16[1024,896]{1,0:T(8,128)(2,1)} %get-tuple-element.102), channel_id=1, source_target_pairs={{0,1},{1,0},{2,3},{3,2},{4,5},{5,4},{6,7},{7,6},{8,9},{9,8},{10,11... | collective-permute-start | bytes 5505032 | tf_op jit(solution)/shard_map/ppermute | solution.py:51
  300.7 49.3 %collective-permute-start.22 = (bf16[1024,896]{1,0:T(8,128)(2,1)}, bf16[1024,896]{1,0:T(8,128)(2,1)}, u32[]{:S(2)}, u32[]{:S(2)}) collective-permute-start(bf16[1024,896]{1,0:T(8,128)(2,1)} %get-tuple-element.81), channel_id=1, source_target_pairs={{0,1},{1,0},{2,3},{3,2},{4,5},{5,4},{6,7},{7,6},{8,9},{9,8},{10,11... | collective-permute-start | bytes 5505032 | tf_op jit(solution)/shard_map/ppermute | solution.py:51
  321.1 49.9 %collective-permute-start.46 = (bf16[4,112,1280]{2,1,0:T(8,128)(2,1)}, bf16[4,112,1280]{2,1,0:T(8,128)(2,1)}, u32[]{:S(2)}, u32[]{:S(2)}) collective-permute-start(bf16[4,112,1280]{2,1,0:T(8,128)(2,1)} %constant_dynamic-slice_fusion), channel_id=1, source_target_pairs={{0,16},{16,0},{1,17},{17,1},{2,18},{18,2},{3,19},{19,3},{4,20},{20... | collective-permute-start | bytes 3440648 | tf_op jit(solution)/shard_map/ppermute | solution.py:51
  348.6 84.5 %collective-permute-start.40 = (bf16[4,112,1280]{2,1,0:T(8,128)(2,1)}, bf16[4,112,1280]{2,1,0:T(8,128)(2,1)}, u32[]{:S(2)}, u32[]{:S(2)}) collective-permute-start(bf16[4,112,1280]{2,1,0:T(8,128)(2,1)} %constant_dynamic-slice_fusion.2), channel_id=1, source_target_pairs={{0,16},{16,0},{1,17},{17,1},{2,18},{18,2},{3,19},{19,3},{4,20},{20... | collective-permute-start | bytes 3440648 | tf_op jit(solution)/shard_map/ppermute | solution.py:51
  353.3 41.7 %collective-permute-start.23 = (bf16[1024,896]{1,0:T(8,128)(2,1)}, bf16[1024,896]{1,0:T(8,128)(2,1)}, u32[]{:S(2)}, u32[]{:S(2)}) collective-permute-start(bf16[1024,896]{1,0:T(8,128)(2,1)} %add_convert_fusion.3), channel_id=1, source_target_pairs={{0,2},{1,3},{2,0},{3,1},{4,6},{5,7},{6,4},{7,5},{8,10},{9,11},{10,... | collective-permute-start | bytes 5505032 | tf_op jit(solution)/shard_map/ppermute | solution.py:51
  370.1 83.3 %collective-permute-start.41 = (bf16[4,112,1280]{2,1,0:T(8,128)(2,1)S(1)}, bf16[4,112,1280]{2,1,0:T(8,128)(2,1)}, u32[]{:S(2)}, u32[]{:S(2)}) collective-permute-start(bf16[4,112,1280]{2,1,0:T(8,128)(2,1)S(1)} %constant_dynamic-slice_fusion.1), channel_id=1, source_target_pairs={{0,16},{16,0},{1,17},{17,1},{2,18},{18,2},{3,19},{19,3},{4,20},{20... | collective-permute-start | bytes 3440648 | tf_op jit(solution)/shard_map/ppermute | solution.py:51
  373.1 35.0 %collective-permute-start.47 = (bf16[112,1280]{1,0:T(8,128)(2,1)S(1)}, bf16[112,1280]{1,0:T(8,128)(2,1)}, u32[]{:S(2)}, u32[]{:S(2)}) collective-permute-start(bf16[112,1280]{1,0:T(8,128)(2,1)S(1)} %dynamic-slice_bitcast_fusion), channel_id=1, source_target_pairs={{0,4},{4,8},{8,12},{12,0},{1,5},{5,9},{9,13},{13,1},{2,6},{6,10},{... | collective-permute-start | bytes 860168 | tf_op jit(solution)/shard_map/ppermute | solution.py:55
  456.1 47.2 %collective-permute-start.42 = (bf16[224,1280]{1,0:T(8,128)(2,1)}, bf16[224,1280]{1,0:T(8,128)(2,1)}, u32[]{:S(2)}, u32[]{:S(2)}) collective-permute-start(bf16[224,1280]{1,0:T(8,128)(2,1)} %fusion.44), channel_id=1, source_target_pairs={{0,4},{4,8},{8,12},{12,0},{1,5},{5,9},{9,13},{13,1},{2,6},{6,10},{... | collective-permute-start | bytes 1720328 | tf_op jit(solution)/shard_map/ppermute | solution.py:55
  487.0 35.2 %collective-permute-start.33 = (bf16[2,896,512]{2,1,0:T(8,128)(2,1)S(1)}, bf16[2,896,512]{2,1,0:T(8,128)(2,1)S(1)}, u32[]{:S(2)}, u32[]{:S(2)}) collective-permute-start(bf16[2,896,512]{2,1,0:T(8,128)(2,1)S(1)} %broadcast_select_fusion), channel_id=1, source_target_pairs={{0,1},{1,0},{2,3},{3,2},{4,5},{5,4},{6,7},{7,6},{8,9},{9,8},{10,11... | collective-permute-start | bytes 5505032 | tf_op jit(solution)/shard_map/ppermute | solution.py:51
  493.0 92.9 %collective-permute-start.24 = (bf16[1024,896]{1,0:T(8,128)(2,1)}, bf16[1024,896]{1,0:T(8,128)(2,1)}, u32[]{:S(2)}, u32[]{:S(2)}) collective-permute-start(bf16[1024,896]{1,0:T(8,128)(2,1)} %get-tuple-element.97), channel_id=1, source_target_pairs={{0,1},{1,0},{2,3},{3,2},{4,5},{5,4},{6,7},{7,6},{8,9},{9,8},{10,11... | collective-permute-start | bytes 5505032 | tf_op jit(solution)/shard_map/ppermute | solution.py:51
  504.5 17.7 %collective-permute-start.43 = (bf16[224,1280]{1,0:T(8,128)(2,1)S(1)}, bf16[224,1280]{1,0:T(8,128)(2,1)S(1)}, u32[]{:S(2)}, u32[]{:S(2)}) collective-permute-start(bf16[224,1280]{1,0:T(8,128)(2,1)S(1)} %fusion.38), channel_id=1, source_target_pairs={{0,4},{4,8},{8,12},{12,0},{1,5},{5,9},{9,13},{13,1},{2,6},{6,10},{... | collective-permute-start | bytes 1720328 | tf_op jit(solution)/shard_map/ppermute | solution.py:55
  507.4 38.4 %collective-permute-start.25 = (bf16[1024,896]{1,0:T(8,128)(2,1)S(1)}, bf16[1024,896]{1,0:T(8,128)(2,1)S(1)}, u32[]{:S(2)}, u32[]{:S(2)}) collective-permute-start(bf16[1024,896]{1,0:T(8,128)(2,1)S(1)} %copy-done.51), channel_id=1, source_target_pairs={{0,1},{1,0},{2,3},{3,2},{4,5},{5,4},{6,7},{7,6},{8,9},{9,8},{10,11... | collective-permute-start | bytes 5505032 | tf_op jit(solution)/shard_map/ppermute | solution.py:51
  508.7 19.6 %collective-permute-start.49 = (bf16[112,1280]{1,0:T(8,128)(2,1)S(1)}, bf16[112,1280]{1,0:T(8,128)(2,1)S(1)}, u32[]{:S(2)}, u32[]{:S(2)}) collective-permute-start(bf16[112,1280]{1,0:T(8,128)(2,1)S(1)} %fusion.52), channel_id=1, source_target_pairs={{0,4},{4,8},{8,12},{12,0},{1,5},{5,9},{9,13},{13,1},{2,6},{6,10},{... | collective-permute-start | bytes 860168 | tf_op jit(solution)/shard_map/ppermute | solution.py:55
  523.1 19.9 %collective-permute-start.34 = (bf16[896,512]{1,0:T(8,128)(2,1)S(1)}, bf16[896,512]{1,0:T(8,128)(2,1)S(1)}, u32[]{:S(2)}, u32[]{:S(2)}) collective-permute-start(bf16[896,512]{1,0:T(8,128)(2,1)S(1)} %select_bitcast_fusion), channel_id=1, source_target_pairs={{0,2},{1,3},{2,0},{3,1},{4,6},{5,7},{6,4},{7,5},{8,10},{9,11},{10,... | collective-permute-start | bytes 2752520 | tf_op jit(solution)/shard_map/ppermute | solution.py:51
  528.3 28.8 %collective-permute-start.50 = (bf16[112,1280]{1,0:T(8,128)(2,1)S(1)}, bf16[112,1280]{1,0:T(8,128)(2,1)S(1)}, u32[]{:S(2)}, u32[]{:S(2)}) collective-permute-start(bf16[112,1280]{1,0:T(8,128)(2,1)S(1)} %fusion.51), channel_id=1, source_target_pairs={{0,16},{16,0},{1,17},{17,1},{2,18},{18,2},{3,19},{19,3},{4,20},{20... | collective-permute-start | bytes 860168 | tf_op jit(solution)/shard_map/ppermute | solution.py:51
  544.6 20.3 %collective-permute-start.45 = (bf16[224,1280]{1,0:T(8,128)(2,1)S(1)}, bf16[224,1280]{1,0:T(8,128)(2,1)S(1)}, u32[]{:S(2)}, u32[]{:S(2)}) collective-permute-start(bf16[224,1280]{1,0:T(8,128)(2,1)S(1)} %fusion.36), channel_id=1, source_target_pairs={{0,16},{16,0},{1,17},{17,1},{2,18},{18,2},{3,19},{19,3},{4,20},{20... | collective-permute-start | bytes 1720328 | tf_op jit(solution)/shard_map/ppermute | solution.py:51
  547.5 38.4 %collective-permute-start.27 = (bf16[1024,896]{1,0:T(8,128)(2,1)}, bf16[1024,896]{1,0:T(8,128)(2,1)}, u32[]{:S(2)}, u32[]{:S(2)}) collective-permute-start(bf16[1024,896]{1,0:T(8,128)(2,1)} %add_convert_fusion.2), channel_id=1, source_target_pairs={{0,2},{1,3},{2,0},{3,1},{4,6},{5,7},{6,4},{7,5},{8,10},{9,11},{10,... | collective-permute-start | bytes 5505032 | tf_op jit(solution)/shard_map/ppermute | solution.py:51
  (78 other events, 658.0 us)

commit v2 on v1

v2 whole, which is shorter than its diff:
```python
import functools

import jax
import jax.numpy as jnp
from jax import lax
from jax.experimental import pallas as pl
from jax.experimental.pallas import tpu as pltpu
from jax.sharding import PartitionSpec as P

QH = 14
KVH = 2
HD = 64
SEQ_LEN = 1024
GROUP = QH // KVH
WIDTH = QH * HD
KV_WIDTH = KVH * HD
QK_WIDTH = WIDTH + KV_WIDTH
QKV = QK_WIDTH + KV_WIDTH

EPS = 1e-06
BASE = 1000000.0
MASKED = -1e30
LANES = 128
BLOCK = 256

NN = (((1,), (0,)), ((), ()))
NT = (((1,), (1,)), ((), ()))
TN = (((0,), (0,)), ((), ()))
VMEM_BYTES = 56 * 1024 * 1024


def dot(left, right, dims=NN):
    return lax.dot_general(left, right, dims, preferred_element_type=jnp.float32)


def low(values):
    return values.astype(jnp.bfloat16)


def add(left, right):
    return low(left.astype(jnp.float32) + right.astype(jnp.float32))


def cost(flops, moved, transcendentals=0):
    return pl.CostEstimate(
        flops=int(flops) // 1000,
        bytes_accessed=int(moved) // 1000,
        transcendentals=int(transcendentals) // 1000,
    )


def flip(values, axis, size, bit):
    return lax.ppermute(values, axis, [(i, i ^ bit) for i in range(size)])


def shift(values, axis, size):
    return lax.ppermute(values, axis, [(i, (i + 1) % size) for i in range(size)])


def join(mine, other, odd, axis):
    first = jnp.where(odd, other, mine)
    second = jnp.where(odd, mine, other)
    return jnp.concatenate([first, second], axis)


def half_of(values, which, axis):
    size = values.shape[axis] // 2
    return lax.dynamic_slice_in_dim(values, which * size, size, axis)


def after(values, done):
    return lax.optimization_barrier((values, done))[0] if jax.tree.leaves(done) else values


class Grid:
    def __init__(self, sizes):
        self.dp, self.row, self.col = sizes["dp"], sizes["row"], sizes["col"]
        self.at_dp = lax.axis_index("dp")
        self.at_row = lax.axis_index("row")
        self.at_col = lax.axis_index("col")
        self.odd_dp = self.at_dp % 2
        self.core = self.at_col % 2
        self.pair = self.at_col // 2

    def gather_half_rows(self, block, axis):
        mine = half_of(block, self.odd_dp, axis)
        pairs = []
        for _ in range(1, self.row):
            mine = shift(mine, "row", self.row)
            pairs.append((mine, flip(mine, "dp", self.dp, 1)))
        return pairs, mine

    def gather_columns(self, block, holds):
        other = flip(block, "col", self.col, 2)
        both = join(block[None], other[None], self.pair == 1, 0)
        size = both.shape[1]
        full = jnp.zeros((2, size * self.row, both.shape[2]), both.dtype)
        full = lax.dynamic_update_slice_in_dim(full, both, self.at_row * size, 1)
        mine = half_of(both, self.odd_dp, 1)
        for step in range(1, self.row):
            mine = shift(mine, "row", self.row)
            mine = after(mine, holds.get(step, ()))
            whole = join(mine, flip(mine, "dp", self.dp, 1), self.odd_dp == 1, 1)
            at = (self.at_row - step) % self.row
            full = lax.dynamic_update_slice_in_dim(full, whole, at * size, 1)
        return full, mine

    def gather_small(self, block):
        size = block.shape[1]
        both = join(block, flip(block, "col", self.col, 2), self.pair == 1, 1)
        other = flip(both, "col", self.col, 1)
        first = jnp.where(self.core == 1, other, both)
        second = jnp.where(self.core == 1, both, other)
        pieces = [first[:, :size], second[:, :size], first[:, size:], second[:, size:]]
        return jnp.concatenate(pieces, 1)

    def swap_halves(self, part):
        size = part.shape[0] // self.row
        blocks = part.reshape(self.row, size, part.shape[1])
        mine = half_of(blocks, self.odd_dp, 1)
        theirs = half_of(blocks, 1 - self.odd_dp, 1)
        return mine, flip(theirs, "dp", self.dp, 1), theirs

    def sum_pairs(self, total):
        bit = 2
        while bit < self.dp:
            total = add(total, flip(total, "dp", self.dp, bit))
            bit *= 2
        return total

    def own_block(self, mine, step):
        at = (self.at_row - step) % self.row
        return lax.dynamic_index_in_dim(mine, at, 0, False)

    def ring_start(self, mine):
        sent = self.own_block(mine, 1)
        return shift(sent, "row", self.row), sent

    def ring_step(self, mine, got, step):
        total = add(got, self.own_block(mine, step + 1))
        if step < self.row - 1:
            return total, shift(total, "row", self.row)
        return self.sum_pairs(total)

    def scatter_direct(self, mine):
        total = lax.dynamic_index_in_dim(mine, self.at_row, 0, False).astype(jnp.float32)
        for step in range(1, self.row):
            to = (self.at_row + step) % self.row
            block = lax.dynamic_index_in_dim(mine, to, 0, False)
            pairs = [(i, (i + step) % self.row) for i in range(self.row)]
            total = total + lax.ppermute(block, "row", pairs).astype(jnp.float32)
        return self.sum_pairs(low(total))

    def sum_axis(self, values, axis):
        size = getattr(self, axis)
        return [
            lax.ppermute(values, axis, [(i, (i + step) % size) for i in range(size)])
            for step in range(1, size)
        ]

    def both_halves(self, total):
        other = flip(total, "dp", self.dp, 1)
        return join(total, other, self.odd_dp == 1, 0)

    def core_parts(self, part):
        size = part.shape[0] // self.col
        pieces = part.reshape(self.col, size, part.shape[1])
        evens, odds = jnp.stack([pieces[0], pieces[2]]), jnp.stack([pieces[1], pieces[3]])
        mine = jnp.where(self.core == 1, odds, evens)
        theirs = jnp.where(self.core == 1, evens, odds)
        return mine, flip(theirs, "col", self.col, 1), theirs

    def pair_parts(self, both):
        mine = jnp.where(self.pair == 1, both[1], both[0])
        theirs = jnp.where(self.pair == 1, both[0], both[1])
        return mine, flip(theirs, "col", self.col, 2), theirs


def turn_pairs(values, cosine, sine):
    lane = lax.broadcasted_iota(jnp.int32, values.shape, 1)
    before = pltpu.roll(values, HD // 2, 1)
    after = pltpu.roll(values, LANES - HD // 2, 1)
    partner = jnp.where(lane % HD < HD // 2, after, before)
    return values * cosine + partner * sine


def place_kernel(joint_size, mine_ref, other_ref, joint_ref, output_ref):
    core = lax.axis_index("col") % 2
    size = mine_ref.shape[2]
    rest = size - joint_size

    def place(first_ref, second_ref):
        pieces = (first_ref[0], second_ref[0], first_ref[1], second_ref[1])
        for j, piece in enumerate(pieces):
            joint_ref[:, j * joint_size : (j + 1) * joint_size] = piece[:, :joint_size]
            output_ref[:, j * rest : (j + 1) * rest] = piece[:, joint_size:]

    @pl.when(core == 0)
    def _():
        place(mine_ref, other_ref)

    @pl.when(core == 1)
    def _():
        place(other_ref, mine_ref)


def place_columns(mine, other, joint_size):
    _, rows, size = mine.shape
    step = rows // 4
    block = pl.BlockSpec((2, step, size), lambda i: (0, i, 0))
    widths = (4 * joint_size, 4 * (size - joint_size))
    return pl.pallas_call(
        functools.partial(place_kernel, joint_size),
        grid=(4,),
        in_specs=[block, block],
        out_specs=[pl.BlockSpec((step, width), lambda i: (i, 0)) for width in widths],
        out_shape=[jax.ShapeDtypeStruct((rows, width), jnp.bfloat16) for width in widths],
        compiler_params=pltpu.CompilerParams(vmem_limit_bytes=VMEM_BYTES),
        cost_estimate=cost(0, 16 * rows * size),
        name="place_columns",
    )(mine, other)


def joint_kernel(x_ref, gain_ref, weight_ref, bias_ref, cos_ref, sin_ref, act_ref, out_ref):
    inputs = x_ref[...].astype(jnp.float32)
    inverse = lax.rsqrt(jnp.mean(inputs * inputs, -1, keepdims=True) + EPS)
    act = low(inputs * inverse * gain_ref[...])
    act_ref[...] = act
    joint = dot(act, weight_ref[...]) + bias_ref[...]
    cosine, sine = cos_ref[...], sin_ref[...]
    for start in range(0, QK_WIDTH, LANES):
        turned = turn_pairs(joint[:, start : start + LANES], cosine, sine)
        out_ref[:, start : start + LANES] = low(turned)
    out_ref[:, QK_WIDTH:] = low(joint[:, QK_WIDTH:])


def joint_projection(inputs, gain, weight, bias, cosine, sine):
    tokens, width = inputs.shape
    steps = SEQ_LEN // BLOCK
    return pl.pallas_call(
        joint_kernel,
        grid=(tokens // BLOCK,),
        in_specs=[
            pl.BlockSpec((BLOCK, width), lambda i: (i, 0)),
            pl.BlockSpec((1, width), lambda i: (0, 0)),
            pl.BlockSpec((width, QKV), lambda i: (0, 0)),
            pl.BlockSpec((1, QKV), lambda i: (0, 0)),
            pl.BlockSpec((BLOCK, LANES), lambda i: (i % steps, 0)),
            pl.BlockSpec((BLOCK, LANES), lambda i: (i % steps, 0)),
        ],
        out_specs=[
            pl.BlockSpec((BLOCK, width), lambda i: (i, 0)),
            pl.BlockSpec((BLOCK, QKV), lambda i: (i, 0)),
        ],
        out_shape=[
            jax.ShapeDtypeStruct((tokens, width), jnp.bfloat16),
            jax.ShapeDtypeStruct((tokens, QKV), jnp.bfloat16),
        ],
        compiler_params=pltpu.CompilerParams(vmem_limit_bytes=VMEM_BYTES),
        cost_estimate=cost(2 * tokens * width * QKV * 2, 8 * tokens * QKV),
        name="joint_projection",
    )(inputs, gain, weight, bias, cosine, sine)


def select_head(values, head):
    return jnp.where(head // GROUP == 0, values[:, :HD], values[:, HD:])


def attend_kernel(first, q_ref, k_ref, v_ref, out_ref):
    pair = pl.program_id(1) + first
    scale = HD ** (-0.5)
    for e in range(2):
        keys = select_head(k_ref[...], 2 * pair + e)
        values = select_head(v_ref[...], 2 * pair + e)
        for i in range(SEQ_LEN // BLOCK):
            rows, end = pl.ds(i * BLOCK, BLOCK), (i + 1) * BLOCK
            query = q_ref[rows, e * HD : (e + 1) * HD] * jnp.bfloat16(scale)
            scores = dot(query, keys[:end], NT)
            rows_at = i * BLOCK + lax.broadcasted_iota(jnp.int32, scores.shape, 0)
            keys_at = lax.broadcasted_iota(jnp.int32, scores.shape, 1)
            scores = jnp.where(keys_at <= rows_at, scores, MASKED)
            weights = jnp.exp(scores - jnp.max(scores, -1, keepdims=True))
            total = jnp.sum(weights, -1, keepdims=True)
            attended = dot(low(weights), values[:end]) / total
            out_ref[rows, e * HD : (e + 1) * HD] = low(attended)


def attend(joint, first, pairs):
    tokens = joint.shape[0]
    seqs = tokens // SEQ_LEN
    return pl.pallas_call(
        functools.partial(attend_kernel, first),
        grid=(seqs, pairs),
        in_specs=[
            pl.BlockSpec((SEQ_LEN, LANES), lambda s, p: (s, p + first)),
            pl.BlockSpec((SEQ_LEN, LANES), lambda s, p: (s, WIDTH // LANES)),
            pl.BlockSpec((SEQ_LEN, LANES), lambda s, p: (s, QK_WIDTH // LANES)),
        ],
        out_specs=pl.BlockSpec((SEQ_LEN, LANES), lambda s, p: (s, p)),
        out_shape=jax.ShapeDtypeStruct((tokens, pairs * LANES), jnp.bfloat16),
        compiler_params=pltpu.CompilerParams(vmem_limit_bytes=VMEM_BYTES),
        cost_estimate=cost(
            tokens * SEQ_LEN * pairs * 1024, 8 * tokens * pairs * LANES, tokens * 1024 * pairs
        ),
        name="attend",
    )(joint, joint, joint)


def attend_back_kernel(first, last, *refs):
    q_ref, k_ref, v_ref, g_ref, cos_ref, sin_ref = refs[:6]
    if first > 0:
        key_in, value_in = refs[7:9]
    ends = last == QH // 2 - 1
    if not ends:
        dk_ref, dv_ref = refs[-4:-2]
    dq_ref = refs[-3] if ends else refs[-5]
    key_sum, value_sum = refs[-2:]
    pair = pl.program_id(1) + first
    scale = HD ** (-0.5)

    @pl.when(pair == first)
    def _():
        key_sum[...] = key_in[...] if first > 0 else jnp.zeros_like(key_sum)
        value_sum[...] = value_in[...] if first > 0 else jnp.zeros_like(value_sum)

    @pl.when(pair <= last)
    def _():
        for i in range(SEQ_LEN // BLOCK):
            rows, end = pl.ds(i * BLOCK, BLOCK), (i + 1) * BLOCK
            parts = []
            for e in range(2):
                head = 2 * pair + e
                kv = head // GROUP
                keys = select_head(k_ref[:end, :], head)
                values = select_head(v_ref[:end, :], head)
                query = q_ref[rows, e * HD : (e + 1) * HD] * jnp.bfloat16(scale)
                grad = g_ref[rows, e * HD : (e + 1) * HD]
                scores = dot(keys, query, NT)
                keys_at = lax.broadcasted_iota(jnp.int32, scores.shape, 0)
                rows_at = i * BLOCK + lax.broadcasted_iota(jnp.int32, scores.shape, 1)
                scores = jnp.where(keys_at <= rows_at, scores, MASKED)
                weights = jnp.exp(scores - jnp.max(scores, 0, keepdims=True))
                prob = weights * (1.0 / jnp.sum(weights, 0, keepdims=True))
                prob_grad = dot(values, grad, NT)
                inner = jnp.sum(prob * prob_grad, 0, keepdims=True)
                score_grad = low(prob * (prob_grad - inner))
                value_sum[kv, :end, :] += dot(low(prob), grad)
                key_sum[kv, :end, :] += dot(score_grad, query)
                parts.append(dot(keys, score_grad, TN))
            query_grad = jnp.transpose(jnp.concatenate(parts, 0)) * scale
            turned = turn_pairs(query_grad, cos_ref[rows, :], -sin_ref[rows, :])
            dq_ref[rows, :] = low(turned)

    if not ends:

        @pl.when(pair == last)
        def _():
            dk_ref[...] = key_sum[...]
            dv_ref[...] = value_sum[...]

        return

    @pl.when(pair == last + 1)
    def _():
        key_grad = jnp.concatenate([key_sum[0], key_sum[1]], 1)
        dq_ref[...] = low(turn_pairs(key_grad, cos_ref[...], -sin_ref[...]))

    @pl.when(pair == last + 2)
    def _():
        dq_ref[...] = low(jnp.concatenate([value_sum[0], value_sum[1]], 1))


def attend_back(joint, grad, cosine, sine, first, pairs, sums):
    tokens = joint.shape[0]
    last = first + pairs - 1
    ends = last == QH // 2 - 1
    seqs = tokens // SEQ_LEN
    steps = pairs + 2 if ends else pairs
    block = (SEQ_LEN, LANES)
    held = pl.BlockSpec((KVH, SEQ_LEN, HD), lambda s, p: (s, 0, 0))
    return pl.pallas_call(
        functools.partial(attend_back_kernel, first, last),
        grid=(seqs, steps),
        in_specs=[
            pl.BlockSpec(block, lambda s, p: (s, jnp.minimum(p + first, last))),
            pl.BlockSpec(block, lambda s, p: (s, WIDTH // LANES)),
            pl.BlockSpec(block, lambda s, p: (s, QK_WIDTH // LANES)),
            pl.BlockSpec(block, lambda s, p: (s, jnp.minimum(p + first, last))),
            pl.BlockSpec(block, lambda s, p: (0, 0)),
            pl.BlockSpec(block, lambda s, p: (0, 0)),
        ]
        + ([pl.BlockSpec(memory_space=pl.ANY), held, held] if sums else []),
        out_specs=[pl.BlockSpec(block, lambda s, p: (s, p + first))]
        + ([] if ends else [held] * 2),
        out_shape=[jax.ShapeDtypeStruct((tokens, QKV), jnp.bfloat16)]
        + [jax.ShapeDtypeStruct((seqs * KVH, SEQ_LEN, HD), jnp.float32)] * (0 if ends else 2),
        input_output_aliases={6: 0} if sums else {},
        scratch_shapes=[
            pltpu.VMEM((KVH, SEQ_LEN, HD), jnp.float32),
            pltpu.VMEM((KVH, SEQ_LEN, HD), jnp.float32),
        ],
        compiler_params=pltpu.CompilerParams(vmem_limit_bytes=VMEM_BYTES),
        cost_estimate=cost(
            tokens * SEQ_LEN * pairs * 2560, 8 * tokens * pairs * LANES, tokens * 1024 * pairs
        ),
        name="attend_back",
    )(joint, joint, joint, grad, cosine, sine, *sums)


def feed_kernel(sizes, held, *refs):
    rows, dps = sizes
    pieces = 2 * rows - 1
    act_ref, cot_ref = refs[:2]
    parts = refs[2 : 2 + pieces]
    outs = refs[2 + pieces + held :]
    mix_ref, grad_ref, hid_ref, dgate_ref, dup_ref, act_out, cot_out, weight_ref, sems = outs
    size = parts[0].shape[1]
    half = size // 2

    @pl.when(pl.program_id(0) == 0)
    def _():
        row, odd = lax.axis_index("row"), lax.axis_index("dp") % 2
        copies = []
        for at, part in enumerate(parts):
            step = (at + 1) // 2
            start = (row + rows - step) % rows * size
            if at > 0:
                start = start + half * (odd if at % 2 == 1 else 1 - odd)
            span = pl.ds(pl.multiple_of(start, 16), part.shape[1])
            copies.append(pltpu.make_async_copy(part, weight_ref.at[:, span, :], sems.at[at]))
        for copy in copies:
            copy.start()
        for copy in copies:
            copy.wait()

    act, cot = act_ref[...], cot_ref[...]
    act_out[...] = act
    cot_out[...] = cot
    gate_ref, up_ref, down_ref = weight_ref.at[0], weight_ref.at[1], weight_ref.at[2]
    gate = dot(act, gate_ref[...])
    up_part = dot(act, up_ref[...])
    hidden_grad = dot(cot, down_ref[...])
    sigma = jax.nn.sigmoid(gate)
    silu = gate * sigma
    hidden = low(silu * up_part)
    gate_grad = low(hidden_grad * up_part * sigma * (1.0 + gate * (1.0 - sigma)))
    up_grad = low(hidden_grad * silu)
    hid_ref[...] = hidden
    dgate_ref[...] = gate_grad
    dup_ref[...] = up_grad
    mix_ref[...] = low(dot(hidden, down_ref[...], NT))
    grad_ref[...] = low(dot(gate_grad, gate_ref[...], NT) + dot(up_grad, up_ref[...], NT))


def feed(sizes, slot, slots, act, cot, parts, held):
    tokens, width = act.shape
    inner = parts[0].shape[2]
    steps = tokens // BLOCK
    narrow = pl.BlockSpec((BLOCK, width), lambda i: (i, 0))
    narrow_at = pl.BlockSpec((BLOCK, width), lambda i: (i + slot * steps, 0))
    wide_at = pl.BlockSpec((BLOCK, inner), lambda i: (i + slot * steps, 0))
    anywhere = pl.BlockSpec(memory_space=pl.ANY)
    first = 2 + len(parts)
    return pl.pallas_call(
        functools.partial(feed_kernel, sizes, len(held)),
        grid=(steps,),
        in_specs=[narrow, narrow] + [anywhere] * (len(parts) + len(held)),
        out_specs=[narrow, narrow, wide_at, wide_at, wide_at, narrow_at, narrow_at],
        out_shape=[jax.ShapeDtypeStruct((tokens, width), jnp.bfloat16)] * 2
        + [jax.ShapeDtypeStruct((slots * tokens, inner), jnp.bfloat16)] * 3
        + [jax.ShapeDtypeStruct((slots * tokens, width), jnp.bfloat16)] * 2,
        scratch_shapes=[
            pltpu.VMEM((3, width, inner), jnp.bfloat16),
            pltpu.SemaphoreType.DMA((len(parts),)),
        ],
        input_output_aliases={first + at: 2 + at for at in range(len(held))},
        compiler_params=pltpu.CompilerParams(vmem_limit_bytes=VMEM_BYTES),
        cost_estimate=cost(
            12 * tokens * width * inner, 2 * tokens * (4 * width + 3 * inner), tokens * inner
        ),
        name="feed",
    )(act, cot, *parts, *held)


def normalize_back(values, inverse, gain, upstream):
    weighted = upstream * gain
    inner = jnp.mean(weighted * values, -1, keepdims=True)
    value_grad = inverse * weighted - values * inverse * inverse * inverse * inner
    gain_grad = jnp.sum(upstream * values * inverse, 0)
    return (value_grad, gain_grad)


def inverse_of(values):
    return lax.rsqrt(jnp.mean(values * values, -1, keepdims=True) + EPS)


def rotary_tables():
    freq = BASE ** (-(jnp.arange(HD // 2, dtype=jnp.float32) * 2.0 / HD))
    angle = jnp.arange(SEQ_LEN, dtype=jnp.float32)[:, None] * freq[None, :]
    cosine, sine = jnp.cos(angle), jnp.sin(angle)
    cosine = jnp.concatenate([cosine] * 4, 1)
    sine = jnp.concatenate([-sine, sine, -sine, sine], 1)
    return cosine, sine


def body(
    sizes,
    block_input,
    first_gain,
    joint_weight,
    joint_bias,
    output_weight,
    second_gain,
    gate_weight,
    up_weight,
    down_weight,
    cotangent,
):
    grid = Grid(sizes)
    shard = gate_weight.shape[1]
    inner = -(-shard // LANES) * LANES
    wide = ((0, 0), (0, inner - shard))
    gain_size, bias_size = first_gain.shape[0], joint_bias.shape[0]
    stretch = (0, bias_size - gain_size)
    size = sizes["col"]
    small = jnp.stack([joint_bias, jnp.pad(first_gain, stretch), jnp.pad(second_gain, stretch)])
    small = grid.gather_small(small.astype(jnp.float32))
    weights = jnp.stack([gate_weight, up_weight, down_weight.T])
    weights = jnp.pad(weights, ((0, 0),) + wide)
    weight_half = half_of(weights, grid.odd_dp, 1)
    columns = after(jnp.concatenate([joint_weight, output_weight], 1), weight_half)
    ring_one = shift(weight_half, "row", sizes["row"])
    mine, last = grid.gather_columns(columns, {1: small, 3: ring_one})
    bias_full = small[0:1]
    first_scale, second_scale = (
        jnp.concatenate(
            [small[k : k + 1, j * bias_size : j * bias_size + gain_size] for j in range(size)], 1
        )
        for k in (1, 2)
    )
    other = flip(mine, "col", size, 1)
    joint_full, output_full = place_columns(mine, other, bias_size)
    cosine, sine = rotary_tables()
    cot_near = flip(cotangent, "col", size, 1)
    cot_far = flip(after(cotangent, last), "col", size, 2)

    first_act, joint = joint_projection(
        block_input, first_scale, joint_full, bias_full, cosine, sine
    )
    rows, pair = sizes["row"], sizes["dp"]
    ring_one = after(ring_one, last)
    rings = [ring_one, shift(ring_one, "row", rows)]
    turned = [flip(ring_one, "dp", pair, 1)]
    attended_low = attend(after(joint, (rings[1], turned[0])), 0, 4)
    rings[1] = after(rings[1], joint)
    rings.append(shift(rings[1], "row", rows))
    turned.append(flip(rings[1], "dp", pair, 1))
    attended_high = attend(after(joint, (rings[2], cot_far)), 4, 3)
    rings[2] = after(rings[2], attended_low)
    turned.append(flip(rings[2], "dp", pair, 1))
    parts = [weights]
    for ring, turn in zip(rings, turned):
        parts += [ring, turn]
    attended = after(jnp.concatenate([attended_low, attended_high], 1), turned)
    inputs = block_input.astype(jnp.float32)
    resid = inputs + dot(attended, output_full)
    second_inverse = inverse_of(resid)
    second_act = low(resid * second_inverse * second_scale)

    act_near = flip(second_act, "col", size, 1)
    act_far = flip(second_act, "col", size, 2)
    cot_last = flip(after(cot_far, attended_low), "col", size, 1)
    parts = [after(part, second_act) for part in parts]
    run = functools.partial(feed, (sizes["row"], sizes["dp"]))
    mix_own, grad_own, *held = run(0, size, second_act, cotangent, parts, ())
    cot_last = after(cot_last, grad_own)
    mix_near, grad_near, *held = run(1, size, act_near, cot_near, parts, held)
    act_far = after(act_far, grad_near)
    act_last = flip(act_far, "col", size, 1)
    mix_last, grad_last, *held = run(2, size, act_last, cot_last, parts, held)
    mix_far, grad_far, *held = run(3, size, act_far, cot_far, parts, held)
    hidden, gate_grad, up_grad, act_all, cot_all = held

    got_near = flip(grad_near, "col", size, 1)
    got_last = flip(grad_last, "col", size, 1)
    far_sum = add(grad_far, after(got_last, grad_far))
    got_far = flip(far_sum, "col", size, 2)

    down_part = low(dot(cot_all, after(hidden, far_sum), TN))
    down_mine = down_part.reshape(sizes["row"], -1, inner)
    down_got, sent = grid.ring_start(down_mine)
    gate_part = low(dot(act_all, after(gate_grad, sent), TN))
    gate_mine, gate_got, sent = grid.swap_halves(gate_part)
    down_total, down_got = grid.ring_step(down_mine, after(down_got, gate_part), 1)
    up_part = low(dot(act_all, after(up_grad, (sent, down_total)), TN))
    up_mine, up_got, sent = grid.swap_halves(up_part)
    got_far = after(got_far, sent)
    second_grad = grad_own.astype(jnp.float32) + got_near.astype(jnp.float32)
    second_grad = second_grad + got_far.astype(jnp.float32)
    resid_norm_grad, second_gain_grad = normalize_back(
        resid, second_inverse, second_scale, second_grad
    )
    resid_grad = cotangent.astype(jnp.float32) + resid_norm_grad
    proj_grad = low(resid_grad)
    attended_grad = low(dot(proj_grad, output_full, NT))
    mix_got = flip(after(mix_last, far_sum), "col", size, 1)
    mix_near = flip(after(mix_near, far_sum), "col", size, 1)
    mix_got = after(mix_got, attended_grad)
    mix_far = flip(add(mix_far, mix_got), "col", size, 2)
    output_part = low(dot(after(proj_grad, attended_grad), attended, TN))
    output_mine, output_got, sent = grid.core_parts(output_part)

    back = functools.partial(attend_back, joint)
    gate_mine = add(gate_mine, after(gate_got, proj_grad))
    gate_got, gate_sent = grid.ring_start(gate_mine)
    down_total, down_got = grid.ring_step(down_mine, after(down_got, proj_grad), 2)
    hold = after(attended_grad, (sent, down_total, gate_sent))
    query_low, *sums = back(hold, cosine, sine, 0, 3, ())

    down_total = grid.ring_step(down_mine, after(down_got, query_low), 3)
    down_got = flip(down_total, "dp", pair, 1)
    gate_total, gate_got = grid.ring_step(gate_mine, after(gate_got, query_low), 1)
    up_mine = add(up_mine, after(up_got, query_low))
    up_got, up_sent = grid.ring_start(up_mine)
    output_mine = add(output_mine, after(output_got, query_low))
    output_mine, output_got, sent = grid.pair_parts(output_mine)
    hold = after(attended_grad, (sent, gate_total, up_sent, down_total))
    query_mid, *sums = back(hold, cosine, sine, 3, 2, (query_low, *sums))

    gate_total, gate_got = grid.ring_step(gate_mine, after(gate_got, query_mid), 2)
    up_total, up_got = grid.ring_step(up_mine, after(up_got, query_mid), 1)
    down_w_grad = add(down_total, after(down_got, query_mid))
    hold = after(attended_grad, (up_total, gate_total, down_w_grad))
    joint_grad = back(hold, cosine, sine, 5, 2, (query_mid, *sums))[0]

    gate_total = grid.ring_step(gate_mine, after(gate_got, joint_grad), 3)
    up_total, up_got = grid.ring_step(up_mine, after(up_got, joint_grad), 2)
    joint_part = low(dot(after(joint_grad, (gate_total, up_total)), first_act, TN))
    gate_w_grad = grid.both_halves(gate_total)
    output_mine = add(output_mine, after(output_got, joint_grad))
    first_grad = dot(after(joint_grad, joint_part), joint_full, NT)
    bias_grad = jnp.sum(joint_grad.astype(jnp.float32), 0)
    first_inverse = inverse_of(inputs)
    input_norm_grad, first_gain_grad = normalize_back(
        inputs, first_inverse, first_scale, first_grad
    )
    input_grad = low(resid_grad + input_norm_grad)
    totals = jnp.concatenate([bias_grad, first_gain_grad, second_gain_grad])
    totals_got = grid.sum_axis(totals, "col")
    joint_mine, joint_got, _ = grid.core_parts(joint_part)
    joint_mine = add(joint_mine, joint_got)
    joint_mine, joint_got, sent = grid.pair_parts(joint_mine)
    up_total = grid.ring_step(up_mine, after(up_got, sent), 3)

    block_grad = jnp.concatenate([add(joint_mine, joint_got), output_mine], 0)
    half = block_grad.shape[0] // 2
    mine = half_of(block_grad, grid.odd_dp, 0)
    theirs = half_of(block_grad, 1 - grid.odd_dp, 0)
    got = flip(theirs, "dp", pair, 1)
    totals = sum(after(totals_got, theirs), totals)
    bit = 1
    while bit < rows:
        totals = totals + flip(totals, "row", rows, bit)
        bit *= 2
    mine = add(mine, got)
    up_w_grad = grid.both_halves(after(up_total, mine))
    totals = sum(grid.sum_axis(after(totals, mine), "dp"), totals)
    blocks = mine.reshape(half, rows, -1)
    block_grad = grid.both_halves(grid.scatter_direct(jnp.transpose(blocks, (1, 0, 2))))
    joint_w_grad, output_w_grad = block_grad[:bias_size].T, block_grad[bias_size:].T

    mix_far = after(mix_far, joint_grad).astype(jnp.float32)
    mixed = mix_own.astype(jnp.float32) + mix_near.astype(jnp.float32) + mix_far
    block_output = low(resid + mixed)

    def own(start, size):
        part = size // grid.col
        return lax.dynamic_slice_in_dim(totals, start + grid.at_col * part, part, 0)

    model = first_gain_grad.shape[0]
    wide_out = lambda values: values.astype(jnp.float32)
    return (
        block_output,
        input_grad,
        own(QKV, model),
        wide_out(joint_w_grad),
        own(0, QK_WIDTH),
        own(QK_WIDTH, KV_WIDTH),
        wide_out(output_w_grad),
        own(QKV + model, model),
        wide_out(gate_w_grad[:, :shard]),
        wide_out(up_w_grad[:, :shard]),
        wide_out(down_w_grad[:, :shard].T),
    )


def solution(mesh):
    tokens = P(("dp", "row", "col"), None)
    return jax.shard_map(
        functools.partial(body, dict(mesh.shape)),
        mesh=mesh,
        in_specs=(
            tokens,
            P("col"),
            P("row", "col"),
            P("col"),
            P("row", "col"),
            P("col"),
            P("row", "col"),
            P("row", "col"),
            P("col", "row"),
            tokens,
        ),
        out_specs=(
            tokens,
            tokens,
            P("col"),
            P("row", "col"),
            P("col"),
            P("col"),
            P("row", "col"),
            P("col"),
            P("row", "col"),
            P("row", "col"),
            P("col", "row"),
        ),
        check_vma=False,
    )
```

time: 599 us -> 471 us (0.79)
  waiting for transfers between devices: 191 us -> 90.2 us
  local copies, waits for them, and re-layouts: 41.7 us -> 19.5 us
  other arithmetic: 75.7 us -> 64.1 us
  matrix products: 62.6 us -> 51.4 us
  starting transfers between devices: 33.6 us -> 44.3 us
  Pallas kernels: 185 us -> 193 us
    ppermute x36 -> x35, waiting for transfers between devices: 114 us -> 47 us  [flip(): return lax.ppermute(values, axis, [(i, i ^ bit) for i in range(size)])]
    ppermute x15, waiting for transfers between devices: 77.1 us -> 40.3 us  [shift(): lax.ppermute(values, axis, [(i, (i + 1) % size) for i in range(size)])]
    convert_element_type x20 -> x24, other arithmetic: 22.6 us -> 42.3 us  [low(): return values.astype(jnp.bfloat16)]
    dot_general x8, matrix products: 62.6 us -> 51.4 us  [dot(): lax.dot_general(left, right, dims, preferred_element_type=jnp.float32)]
    concatenate x5 -> x6, other arithmetic: 13.9 us -> 3.09 us  [the longest x1 1.76 us: body(): attended = after(jnp.concatenate([attended_low, attended_high], 1), turned)]
    ppermute x15, starting transfers between devices: 4.86 us -> 14.6 us  [shift(): lax.ppermute(values, axis, [(i, (i + 1) % size) for i in range(size)])]
    pallas_call x4 -> x5, Pallas kernels: 91.2 us -> 100 us  [the longest x4 95.3 us: feed(): pl.pallas_call(functools.partial(feed_kernel, sizes, len(held)), grid=(st...]
    select_n x10 -> x8, other arithmetic: 6.38 us -> 0.26 us  [join(): first = jnp.where(odd, other, mine)]
  transfers between devices with their start and end apart: 51 -> 57, of which waited for: 21 -> 17; matrix products, arithmetic and copies ran while one was open for 28% -> 27% of each run, Pallas kernels for 31% -> 36%
where the time goes in v2:
time: 471 us; the launch traced here: 464 us
  Pallas kernels  193 us (41%)
  waiting for transfers between devices  90.2 us (19%)
  other arithmetic  64.1 us (14%)
  matrix products  51.4 us (11%)
  starting transfers between devices  44.3 us (9%)
  local copies, waits for them, and re-layouts  19.5 us (4%)
    pallas_call x4, Pallas kernels, feed(): pl.pallas_call(functools.partial(feed_kernel, sizes, len(held)), grid=(st...  95.3 us
    pallas_call x3, Pallas kernels, attend_back(): pl.pallas_call(functools.partial(attend_back_kernel, first, last), grid=(...  56.3 us
    dot_general x8, matrix products, dot(): lax.dot_general(left, right, dims, preferred_element_type=jnp.float32)  51.4 us
    ppermute x35, waiting for transfers between devices, flip(): return lax.ppermute(values, axis, [(i, i ^ bit) for i in range(size)])  47 us
    convert_element_type x24, other arithmetic, low(): return values.astype(jnp.bfloat16)  42.3 us
    ppermute x15, waiting for transfers between devices, shift(): lax.ppermute(values, axis, [(i, (i + 1) % size) for i in range(size)])  40.3 us
    pallas_call x2, Pallas kernels, attend(): pl.pallas_call(functools.partial(attend_kernel, first), grid=(seqs, pairs...  29.2 us
    ppermute x35, starting transfers between devices, flip(): return lax.ppermute(values, axis, [(i, i ^ bit) for i in range(size)])  23.8 us
  transfers between devices with their start and end apart: 57, of which 17 were waited for; matrix products, arithmetic and copies ran while one was open for 27% of the time, Pallas kernels for 36%

profile of v2, /device:TPU:0, one launch (start us, length us, event | category | flops | bytes accessed | tf_op | source)
XLA Modules:
  0.0 464.4 jit_solution(12739822242803848394)
XLA Ops:
  10.9 6.2 %collective-permute-done.2 = bf16[224,512]{1,0:T(8,128)(2,1)S(1)} collective-permute-done((bf16[224,512]{1,0:T(8,128)(2,1)S(1)}, bf16[224,512]{1,0:T(8,128)(2,1)S(1)}, u32[]{:S(2)}, u32[]{:S(2)}) %collective-permute-start.2) | collective-permute-done | bytes 229408 | tf_op jit(solution)/shard_map/ppermute | solution.py:53
  19.1 16.9 %collective-permute-done.3 = bf16[2,112,512]{2,1,0:T(8,128)(2,1)S(1)} collective-permute-done((bf16[2,112,512]{2,1,0:T(8,128)(2,1)S(1)}, bf16[2,112,512]{2,1,0:T(8,128)(2,1)S(1)}, u32[]{:S(2)}, u32[]{:S(2)}) %collective-permute-start.3) | collective-permute-done | bytes 229408 | tf_op jit(solution)/shard_map/ppermute | solution.py:57
  37.6 6.4 %collective-permute-done.5 = bf16[2,112,512]{2,1,0:T(8,128)(2,1)S(1)} collective-permute-done((bf16[2,112,512]{2,1,0:T(8,128)(2,1)S(1)}, bf16[2,112,512]{2,1,0:T(8,128)(2,1)S(1)}, u32[]{:S(2)}, u32[]{:S(2)}) %collective-permute-start.5) | collective-permute-done | bytes 229408 | tf_op jit(solution)/shard_map/ppermute | solution.py:57
  45.6 7.7 %collective-permute-done.7 = bf16[2,112,512]{2,1,0:T(8,128)(2,1)S(1)} collective-permute-done((bf16[2,112,512]{2,1,0:T(8,128)(2,1)S(1)}, bf16[2,112,512]{2,1,0:T(8,128)(2,1)S(1)}, u32[]{:S(2)}, u32[]{:S(2)}) %collective-permute-start.7) | collective-permute-done | bytes 229408 | tf_op jit(solution)/shard_map/ppermute | solution.py:57
  53.9 5.4 %collective-permute-done.9 = bf16[2,112,512]{2,1,0:T(8,128)(2,1)S(1)} collective-permute-done((bf16[2,112,512]{2,1,0:T(8,128)(2,1)S(1)}, bf16[2,112,512]{2,1,0:T(8,128)(2,1)S(1)}, u32[]{:S(2)}, u32[]{:S(2)}) %collective-permute-start.9) | collective-permute-done | bytes 229408 | tf_op jit(solution)/shard_map/ppermute | solution.py:53
  66.0 5.0 %place_columns.1 = (bf16[896,1152]{1,0:T(8,128)(2,1)}, bf16[896,896]{1,0:T(8,128)(2,1)}) custom-call(bf16[2,896,512]{2,1,0:T(8,128)(2,1)} %copy-done.14, bf16[2,896,512]{2,1,0:T(8,128)(2,1)} %collective-permute-done.10.other_ref), custom_call_target="tpu_custom_call" | custom-call | bytes 7340 | tf_op jit(solution)/shard_map/place_columns/pallas_call | solution.py:212
  71.0 7.4 %joint_projection.1 = (bf16[1024,896]{1,0:T(8,128)(2,1)}, bf16[1024,1152]{1,0:T(8,128)(2,1)}) custom-call(bf16[1024,896]{1,0:T(8,128)(2,1)} %x_ref.1, f32[1,896]{1,0:T(1,128)} %get-tuple-element.222.gain_ref, bf16[896,1152]{1,0:T(8,128)(2,1)} %get-tuple-element.106.weight_ref, f32[1,1152]{1,0:T(1,128)} %slice.172.bias_ref, ...), custom_call_target="tpu_custom_call" | custom-call | flops 4227858 | bytes 9437 | tf_op jit(solution)/shard_map/joint_projection/pallas_call | solution.py:240
  78.4 4.4 collective-permute-done.11.refs_5_
  87.2 16.5 %attend.2 = bf16[1024,512]{1,0:T(8,128)(2,1)} custom-call(bf16[1024,1152]{1,0:T(8,128)(2,1)} %get-tuple-element.109.q_ref.k_ref.v_ref.refs_0_.refs_1_.refs_2_, bf16[1024,1152]{1,0:T(8,128)(2,1)} %get-tuple-element.109.q_ref.k_ref.v_ref.refs_0_.refs_1_.refs_2_, bf16[1024,1152]{1,0:T(8,128)(2,1)} %get-tuple-element.109.q_ref.k_ref.v_ref.refs_0_.refs_1_.refs_2_), custom_call_target="tpu_custom_call" | custom-call | flops 4294967 | bytes 4194 | tf_op jit(solution)/shard_map/attend/pallas_call | solution.py:291
  106.5 12.6 %attend.3 = bf16[1024,384]{1,0:T(8,128)(2,1)} custom-call(bf16[1024,1152]{1,0:T(8,128)(2,1)} %get-tuple-element.109.q_ref.k_ref.v_ref.refs_0_.refs_1_.refs_2_, bf16[1024,1152]{1,0:T(8,128)(2,1)} %get-tuple-element.109.q_ref.k_ref.v_ref.refs_0_.refs_1_.refs_2_, bf16[1024,1152]{1,0:T(8,128)(2,1)} %get-tuple-element.109.q_ref.k_ref.v_ref.refs_0_.refs_1_.refs_2_), custom_call_target="tpu_custom_call" | custom-call | flops 3221225 | bytes 3145 | tf_op jit(solution)/shard_map/attend/pallas_call | solution.py:291
  120.9 4.7 %collective-permute-done.16.refs_8_ = bf16[3,112,1280]{2,1,0:T(8,128)(2,1)S(1)} collective-permute-done((bf16[3,112,1280]{2,1,0:T(8,128)(2,1)S(1)}, bf16[3,112,1280]{2,1,0:T(8,128)(2,1)S(1)}, u32[]{:S(2)}, u32[]{:S(2)}) %collective-permute-start.16) | collective-permute-done | bytes 860192 | tf_op jit(solution)/shard_map/ppermute | solution.py:53
  131.1 23.9 %feed.4 = (bf16[1024,896]{1,0:T(8,128)(2,1)}, bf16[1024,896]{1,0:T(8,128)(2,1)}, bf16[4096,1280]{1,0:T(8,128)(2,1)}, bf16[4096,1280]{1,0:T(8,128)(2,1)}, bf16[40...) custom-call(bf16[1024,896]{1,0:T(8,128)(2,1)} %copy-done.15, bf16[1024,896]{1,0:T(8,128)(2,1)} %refs_1_.1, ...), custom_call_target="tpu_custom_call" | custom-call | flops 14092861 | bytes 15204 | tf_op jit(solution)/shard_map/feed/pallas_call | solution.py:464
  154.9 23.8 %feed.5 = (bf16[1024,896]{1,0:T(8,128)(2,1)}, bf16[1024,896]{1,0:T(8,128)(2,1)}, bf16[4096,1280]{1,0:T(8,128)(2,1)}, bf16[4096,1280]{1,0:T(8,128)(2,1)}, bf16[40...) custom-call(bf16[1024,896]{1,0:T(8,128)(2,1)} %collective-permute-do, ...), custom_call_target="tpu_custom_call", output_to_operand_aliasing={{2}: (9, {}), {3}: (10, {}), {4}: (11, {}), {5}: (12, {}), ... | custom-call | flops 14092861 | bytes 15204 | tf_op jit(solution)/shard_map/feed/pallas_call | solution.py:464
  178.8 4.0 collective-permute-done.20.refs_0_
  184.0 23.7 %feed.6 = (bf16[1024,896]{1,0:T(8,128)(2,1)}, bf16[1024,896]{1,0:T(8,128)(2,1)}, bf16[4096,1280]{1,0:T(8,128)(2,1)}, bf16[4096,1280]{1,0:T(8,128)(2,1)}, bf16[40...) custom-call(bf16[1024,896]{1,0:T(8,128)(2,1)} %copy-done.33, ...), custom_call_target="tpu_custom_call", output_to_operand_aliasing={{2}: (9, {}), {3}: (10, {}), {4}: (11, {}), {5}: (12, {}), ... | custom-call | flops 14092861 | bytes 15204 | tf_op jit(solution)/shard_map/feed/pallas_call | solution.py:464
  208.8 23.9 %feed.7 = (bf16[1024,896]{1,0:T(8,128)(2,1)}, bf16[1024,896]{1,0:T(8,128)(2,1)}, bf16[4096,1280]{1,0:T(8,128)(2,1)}, bf16[4096,1280]{1,0:T(8,128)(2,1)}, bf16[40...) custom-call(bf16[1024,896]{1,0:T(8,128)(2,1)} %collective-permute-do, ...), custom_call_target="tpu_custom_call", output_to_operand_aliasing={{2}: (9, {}), {3}: (10, {}), {4}: (11, {}), {5}: (12, {}), ... | custom-call | flops 14092861 | bytes 15204 | tf_op jit(solution)/shard_map/feed/pallas_call | solution.py:464
  232.8 3.9 add_convert_fusion.2
  237.8 14.0 %convolution_convert_fusion.3 = bf16[896,1280]{1,0:T(8,128)(2,1)S(1)} fusion(bf16[4096,896]{1,0:T(8,128)(2,1)} %get-tuple-element.155, bf16[4096,1280]{1,0:T(8,128)(2,1)} %get-tuple-element.157), kind=kOutput, calls=%fused_computation.28 | convolution fusion | flops 9396387840 | bytes 20119552 | tf_op jit(solution)/shard_map/dot_general | solution.py:33
  254.5 11.6 %convolution_convert_fusion.2 = bf16[896,1280]{1,0:T(8,128)(2,1)} fusion(bf16[4096,896]{1,0:T(8,128)(2,1)S(1)} %bitcast.108, bf16[4096,1280]{1,0:T(8,128)(2,1)S(1)} %bitcast.104), kind=kOutput, calls=%fused_computation.27 | convolution fusion | flops 9396387840 | bytes 20119552 | tf_op jit(solution)/shard_map/dot_general | solution.py:33
  274.1 10.3 %convolution_convert_fusion.1 = bf16[896,1280]{1,0:T(8,128)(2,1)S(1)} fusion(bf16[4096,896]{1,0:T(8,128)(2,1)S(1)} %bitcast.108, bf16[4096,1280]{1,0:T(8,128)(2,1)S(1)} %bitcast.106), kind=kOutput, calls=%fused_computation.26 | convolution fusion | flops 9396387840 | bytes 20119552 | tf_op jit(solution)/shard_map/dot_general | solution.py:33
  287.2 3.7 multiply_reduce_fusion
  290.9 3.6 fusion.39
  294.6 3.5 convolution_convert_fusion.4.refs_3_
  309.7 22.5 %attend_back.3 = (bf16[1024,1152]{1,0:T(8,128)(2,1)}, f32[2,1024,64]{2,1,0:T(8,128)}, f32[2,1024,64]{2,1,0:T(8,128)}) custom-call(bf16[1024,1152]{1,0:T(8,128)(2,1)} %get-tuple-element.109.q_ref.k_ref.v_ref.refs_0_.refs_1_.refs_2_, bf16[1024,1152]{1,0:T(8,128)(2,1)} %get-tuple-element.109.q_ref.k_ref.v_ref.refs_0_.refs_1_.refs_2_, ...), custom_call_target="tpu_custom_call" | custom-call | flops 8053063 | bytes 3145 | tf_op jit(solution)/shard_map/attend_back/pallas_call | solution.py:381
  332.2 3.9 add_convert_fusion.1
  350.1 16.7 %attend_back.4 = (bf16[1024,1152]{1,0:T(8,128)(2,1)}, f32[2,1024,64]{2,1,0:T(8,128)}, f32[2,1024,64]{2,1,0:T(8,128)}) custom-call(bf16[1024,1152]{1,0:T(8,128)(2,1)} %get-tuple-element.109.q_ref.k_ref.v_ref.refs_0_.refs_1_.refs_2_, bf16[1024,1152]{1,0:T(8,128)(2,1)} %get-tuple-element.109.q_ref.k_ref.v_ref.refs_0_.refs_1_.refs_2_, ...), custom_call_target="tpu_custom_call", output_to_operand_aliasing={{0}: (6, {})} | custom-call | flops 5368709 | bytes 2097 | tf_op jit(solution)/shard_map/attend_back/pallas_call | solution.py:381
  373.8 17.0 %attend_back.5 = bf16[1024,1152]{1,0:T(8,128)(2,1)} custom-call(bf16[1024,1152]{1,0:T(8,128)(2,1)} %get-tuple-element.109.q_ref.k_ref.v_ref.refs_0_.refs_1_.refs_2_, bf16[1024,1152]{1,0:T(8,128)(2,1)} %get-tuple-element.109.q_ref.k_ref.v_ref.refs_0_.refs_1_.refs_2_, ...), custom_call_target="tpu_custom_call", output_to_operand_aliasing={{}: (6, {})} | custom-call | flops 5368709 | bytes 2097 | tf_op jit(solution)/shard_map/attend_back/pallas_call | solution.py:381
  395.2 4.2 convolution_convert_fusion
  412.6 11.1 %collective-permute-done.44 = bf16[288,896]{1,0:T(8,128)(2,1)S(1)} collective-permute-done((bf16[288,896]{1,0:T(8,128)(2,1)S(1)}, bf16[288,896]{1,0:T(8,128)(2,1)S(1)}, u32[]{:S(2)}, u32[]{:S(2)}) %collective-permute-start.44) | collective-permute-done | bytes 516128 | tf_op jit(solution)/shard_map/ppermute | solution.py:53
  430.7 5.0 %collective-permute-done.46 = f32[2944]{0:T(1024)S(1)} collective-permute-done((f32[2944]{0:T(1024)S(1)}, f32[2944]{0:T(1024)S(1)}, u32[]{:S(2)}, u32[]{:S(2)}) %collective-permute-start.46) | collective-permute-done | bytes 11808 | tf_op jit(solution)/shard_map/ppermute | solution.py:53
  436.3 3.6 collective-permute-done.48
  443.1 5.1 %add_convert_fusion = bf16[1024,896]{1,0:T(8,128)(2,1)} fusion(f32[1024,896]{1,0:T(8,128)} %copy-done, bf16[1024,896]{1,0:T(8,128)(2,1)} %collective-permute-done.28, bf16[1024,896]{1,0:T(8,128)(2,1)} %collective-permute-done.23, bf16[1024,896]{1,0:T(8,128)(2,1)S(1)} %copy-done.32), kind=kLoop, calls=%fused_computation.17 | loop fusion | flops 6422528 | bytes 11010048 | tf_op jit(solution)/shard_map/convert_element_type | solution.py:37
  (291 shorter events, 130.4 us)
Async XLA Ops:
  8.4 37.2 %collective-permute-start.8 = (bf16[3,112,1280]{2,1,0:T(8,128)(2,1)}, bf16[3,112,1280]{2,1,0:T(8,128)(2,1)S(1)}, u32[]{:S(2)}, u32[]{:S(2)}) collective-permute-start(bf16[3,112,1280]{2,1,0:T(8,128)(2,1)} %constant_dynamic-slice_fusion.2), channel_id=1, source_target_pairs={{0,4},{4,8},{8,12},{12,0},{1,5},{5,9},{9,13},{13,1},{2,6},{6,10},{... | collective-permute-start | bytes 2580488 | tf_op jit(solution)/shard_map/ppermute | solution.py:57
  17.2 18.8 %collective-permute-start.3 = (bf16[2,112,512]{2,1,0:T(8,128)(2,1)S(1)}, bf16[2,112,512]{2,1,0:T(8,128)(2,1)S(1)}, u32[]{:S(2)}, u32[]{:S(2)}) collective-permute-start(bf16[2,112,512]{2,1,0:T(8,128)(2,1)S(1)} %fusion.33), channel_id=1, source_target_pairs={{0,4},{4,8},{8,12},{12,0},{1,5},{5,9},{9,13},{13,1},{2,6},{6,10},{... | collective-permute-start | bytes 688136 | tf_op jit(solution)/shard_map/ppermute | solution.py:57
  59.5 23.3 %collective-permute-start.11 = (bf16[3,112,1280]{2,1,0:T(8,128)(2,1)S(1)}, bf16[3,112,1280]{2,1,0:T(8,128)(2,1)S(1)}, u32[]{:S(2)}, u32[]{:S(2)}) collective-permute-start(bf16[3,112,1280]{2,1,0:T(8,128)(2,1)S(1)} %collective-permute-done.8.refs_3_), channel_id=1, source_target_pairs={{0,4},{4,8},{8,12},{12,0},{1,5},{5,9},{9,13},{13,1},{2,6},{6,10},{... | collective-permute-start | bytes 2580488 | tf_op jit(solution)/shard_map/ppermute | solution.py:57
  64.0 42.5 %collective-permute-start.14 = (bf16[1024,896]{1,0:T(8,128)(2,1)S(1)}, bf16[1024,896]{1,0:T(8,128)(2,1)}, u32[]{:S(2)}, u32[]{:S(2)}) collective-permute-start(bf16[1024,896]{1,0:T(8,128)(2,1)S(1)} %copy-done.11), channel_id=1, source_target_pairs={{0,2},{1,3},{2,0},{3,1},{4,6},{5,7},{6,4},{7,5},{8,10},{9,11},{10,... | collective-permute-start | bytes 5505032 | tf_op jit(solution)/shard_map/ppermute | solution.py:53
  65.2 22.0 %collective-permute-start.12 = (bf16[3,112,1280]{2,1,0:T(8,128)(2,1)S(1)}, bf16[3,112,1280]{2,1,0:T(8,128)(2,1)S(1)}, u32[]{:S(2)}, u32[]{:S(2)}) collective-permute-start(bf16[3,112,1280]{2,1,0:T(8,128)(2,1)S(1)} %collective-permute-done.8.refs_3_), channel_id=1, source_target_pairs={{0,16},{16,0},{1,17},{17,1},{2,18},{18,2},{3,19},{19,3},{4,20},{20... | collective-permute-start | bytes 2580488 | tf_op jit(solution)/shard_map/ppermute | solution.py:53
  82.8 23.0 %collective-permute-start.13 = (bf16[3,112,1280]{2,1,0:T(8,128)(2,1)S(1)}, bf16[3,112,1280]{2,1,0:T(8,128)(2,1)S(1)}, u32[]{:S(2)}, u32[]{:S(2)}) collective-permute-start(bf16[3,112,1280]{2,1,0:T(8,128)(2,1)S(1)} %collective-permute-done.11.refs_5_), channel_id=1, source_target_pairs={{0,4},{4,8},{8,12},{12,0},{1,5},{5,9},{9,13},{13,1},{2,6},{6,10},{... | collective-permute-start | bytes 2580488 | tf_op jit(solution)/shard_map/ppermute | solution.py:57
  83.3 37.6 %collective-permute-start.15 = (bf16[3,112,1280]{2,1,0:T(8,128)(2,1)S(1)}, bf16[3,112,1280]{2,1,0:T(8,128)(2,1)S(1)}, u32[]{:S(2)}, u32[]{:S(2)}) collective-permute-start(bf16[3,112,1280]{2,1,0:T(8,128)(2,1)S(1)} %collective-permute-done.11.refs_5_), channel_id=1, source_target_pairs={{0,16},{16,0},{1,17},{17,1},{2,18},{18,2},{3,19},{19,3},{4,20},{20... | collective-permute-start | bytes 2580488 | tf_op jit(solution)/shard_map/ppermute | solution.py:53
  105.8 19.8 %collective-permute-start.16 = (bf16[3,112,1280]{2,1,0:T(8,128)(2,1)S(1)}, bf16[3,112,1280]{2,1,0:T(8,128)(2,1)S(1)}, u32[]{:S(2)}, u32[]{:S(2)}) collective-permute-start(bf16[3,112,1280]{2,1,0:T(8,128)(2,1)S(1)} %collective-permute-done.13.refs_7_), channel_id=1, source_target_pairs={{0,16},{16,0},{1,17},{17,1},{2,18},{18,2},{3,19},{19,3},{4,20},{20... | collective-permute-start | bytes 2580488 | tf_op jit(solution)/shard_map/ppermute | solution.py:53
  106.3 48.6 %collective-permute-start.18 = (bf16[1024,896]{1,0:T(8,128)(2,1)S(1)}, bf16[1024,896]{1,0:T(8,128)(2,1)}, u32[]{:S(2)}, u32[]{:S(2)}) collective-permute-start(bf16[1024,896]{1,0:T(8,128)(2,1)S(1)} %copy-done.11), channel_id=1, source_target_pairs={{0,1},{1,0},{2,3},{3,2},{4,5},{5,4},{6,7},{7,6},{8,9},{9,8},{10,11... | collective-permute-start | bytes 5505032 | tf_op jit(solution)/shard_map/ppermute | solution.py:53
  129.8 25.1 %collective-permute-start.17 = (bf16[1024,896]{1,0:T(8,128)(2,1)S(1)}, bf16[1024,896]{1,0:T(8,128)(2,1)}, u32[]{:S(2)}, u32[]{:S(2)}) collective-permute-start(bf16[1024,896]{1,0:T(8,128)(2,1)S(1)} %multiply_convert_fusion.refs_0_), channel_id=1, source_target_pairs={{0,1},{1,0},{2,3},{3,2},{4,5},{5,4},{6,7},{7,6},{8,9},{9,8},{10,11... | collective-permute-start | bytes 5505032 | tf_op jit(solution)/shard_map/ppermute | solution.py:53
  129.8 48.9 %collective-permute-start.19 = (bf16[1024,896]{1,0:T(8,128)(2,1)S(1)}, bf16[1024,896]{1,0:T(8,128)(2,1)}, u32[]{:S(2)}, u32[]{:S(2)}) collective-permute-start(bf16[1024,896]{1,0:T(8,128)(2,1)S(1)} %multiply_convert_fusion.refs_0_), channel_id=1, source_target_pairs={{0,2},{1,3},{2,0},{3,1},{4,6},{5,7},{6,4},{7,5},{8,10},{9,11},{10,... | collective-permute-start | bytes 5505032 | tf_op jit(solution)/shard_map/ppermute | solution.py:53
  130.3 48.5 %collective-permute-start.21 = (bf16[1024,896]{1,0:T(8,128)(2,1)}, bf16[1024,896]{1,0:T(8,128)(2,1)}, u32[]{:S(2)}, u32[]{:S(2)}) collective-permute-start(bf16[1024,896]{1,0:T(8,128)(2,1)} %collective-permute-done.14.refs_1_), channel_id=1, source_target_pairs={{0,1},{1,0},{2,3},{3,2},{4,5},{5,4},{6,7},{7,6},{8,9},{9,8},{10,11... | collective-permute-start | bytes 5505032 | tf_op jit(solution)/shard_map/ppermute | solution.py:53
  207.8 25.0 %collective-permute-start.22 = (bf16[1024,896]{1,0:T(8,128)(2,1)}, bf16[1024,896]{1,0:T(8,128)(2,1)}, u32[]{:S(2)}, u32[]{:S(2)}) collective-permute-start(bf16[1024,896]{1,0:T(8,128)(2,1)} %get-tuple-element.146), channel_id=1, source_target_pairs={{0,1},{1,0},{2,3},{3,2},{4,5},{5,4},{6,7},{7,6},{8,9},{9,8},{10,11... | collective-permute-start | bytes 5505032 | tf_op jit(solution)/shard_map/ppermute | solution.py:53
  208.4 77.7 %collective-permute-start.25 = (bf16[1024,896]{1,0:T(8,128)(2,1)}, bf16[1024,896]{1,0:T(8,128)(2,1)}, u32[]{:S(2)}, u32[]{:S(2)}) collective-permute-start(bf16[1024,896]{1,0:T(8,128)(2,1)} %get-tuple-element.130), channel_id=1, source_target_pairs={{0,1},{1,0},{2,3},{3,2},{4,5},{5,4},{6,7},{7,6},{8,9},{9,8},{10,11... | collective-permute-start | bytes 5505032 | tf_op jit(solution)/shard_map/ppermute | solution.py:53
  236.7 48.8 %collective-permute-start.26 = (bf16[1024,896]{1,0:T(8,128)(2,1)}, bf16[1024,896]{1,0:T(8,128)(2,1)}, u32[]{:S(2)}, u32[]{:S(2)}) collective-permute-start(bf16[1024,896]{1,0:T(8,128)(2,1)} %add_convert_fusion.2), channel_id=1, source_target_pairs={{0,2},{1,3},{2,0},{3,1},{4,6},{5,7},{6,4},{7,5},{8,10},{9,11},{10,... | collective-permute-start | bytes 5505032 | tf_op jit(solution)/shard_map/ppermute | solution.py:53
  237.8 70.2 %collective-permute-start.24 = (bf16[1024,896]{1,0:T(8,128)(2,1)}, bf16[1024,896]{1,0:T(8,128)(2,1)}, u32[]{:S(2)}, u32[]{:S(2)}) collective-permute-start(bf16[1024,896]{1,0:T(8,128)(2,1)} %get-tuple-element.151), channel_id=1, source_target_pairs={{0,1},{1,0},{2,3},{3,2},{4,5},{5,4},{6,7},{7,6},{8,9},{9,8},{10,11... | collective-permute-start | bytes 5505032 | tf_op jit(solution)/shard_map/ppermute | solution.py:53
  254.0 17.9 %collective-permute-start.27 = (bf16[224,1280]{1,0:T(8,128)(2,1)}, bf16[224,1280]{1,0:T(8,128)(2,1)}, u32[]{:S(2)}, u32[]{:S(2)}) collective-permute-start(bf16[224,1280]{1,0:T(8,128)(2,1)} %dynamic-slice_bitcast_fusion), channel_id=1, source_target_pairs={{0,4},{4,8},{8,12},{12,0},{1,5},{5,9},{9,13},{13,1},{2,6},{6,10},{... | collective-permute-start | bytes 1720328 | tf_op jit(solution)/shard_map/ppermute | solution.py:57
  268.4 31.8 %collective-permute-start.31 = (bf16[4,112,1280]{2,1,0:T(8,128)(2,1)}, bf16[4,112,1280]{2,1,0:T(8,128)(2,1)}, u32[]{:S(2)}, u32[]{:S(2)}) collective-permute-start(bf16[4,112,1280]{2,1,0:T(8,128)(2,1)} %constant_dynamic-slice_fusion.1), channel_id=1, source_target_pairs={{0,16},{16,0},{1,17},{17,1},{2,18},{18,2},{3,19},{19,3},{4,20},{20... | collective-permute-start | bytes 3440648 | tf_op jit(solution)/shard_map/ppermute | solution.py:53
  271.9 170.9 %collective-permute-start.23 = (bf16[1024,896]{1,0:T(8,128)(2,1)}, bf16[1024,896]{1,0:T(8,128)(2,1)}, u32[]{:S(2)}, u32[]{:S(2)}) collective-permute-start(bf16[1024,896]{1,0:T(8,128)(2,1)} %get-tuple-element.148), channel_id=1, source_target_pairs={{0,1},{1,0},{2,3},{3,2},{4,5},{5,4},{6,7},{7,6},{8,9},{9,8},{10,11... | collective-permute-start | bytes 5505032 | tf_op jit(solution)/shard_map/ppermute | solution.py:53
  285.5 50.6 %collective-permute-start.29 = (bf16[4,112,1280]{2,1,0:T(8,128)(2,1)}, bf16[4,112,1280]{2,1,0:T(8,128)(2,1)}, u32[]{:S(2)}, u32[]{:S(2)}) collective-permute-start(bf16[4,112,1280]{2,1,0:T(8,128)(2,1)} %constant_dynamic-slice_fusion), channel_id=1, source_target_pairs={{0,16},{16,0},{1,17},{17,1},{2,18},{18,2},{3,19},{19,3},{4,20},{20... | collective-permute-start | bytes 3440648 | tf_op jit(solution)/shard_map/ppermute | solution.py:53
  286.1 19.1 %collective-permute-start.30 = (bf16[224,1280]{1,0:T(8,128)(2,1)}, bf16[224,1280]{1,0:T(8,128)(2,1)S(1)}, u32[]{:S(2)}, u32[]{:S(2)}) collective-permute-start(bf16[224,1280]{1,0:T(8,128)(2,1)} %fusion.17), channel_id=1, source_target_pairs={{0,4},{4,8},{8,12},{12,0},{1,5},{5,9},{9,13},{13,1},{2,6},{6,10},{... | collective-permute-start | bytes 1720328 | tf_op jit(solution)/shard_map/ppermute | solution.py:57
  305.2 42.0 %collective-permute-start.33 = (bf16[2,224,896]{2,1,0:T(8,128)(2,1)}, bf16[2,224,896]{2,1,0:T(8,128)(2,1)}, u32[]{:S(2)}, u32[]{:S(2)}) collective-permute-start(bf16[2,224,896]{2,1,0:T(8,128)(2,1)} %broadcast_select_fusion.1), channel_id=1, source_target_pairs={{0,1},{1,0},{2,3},{3,2},{4,5},{5,4},{6,7},{7,6},{8,9},{9,8},{10,11... | collective-permute-start | bytes 2408456 | tf_op jit(solution)/shard_map/ppermute | solution.py:53
  305.8 33.6 %collective-permute-start.34 = (bf16[112,1280]{1,0:T(8,128)(2,1)S(1)}, bf16[112,1280]{1,0:T(8,128)(2,1)}, u32[]{:S(2)}, u32[]{:S(2)}) collective-permute-start(bf16[112,1280]{1,0:T(8,128)(2,1)S(1)} %dynamic-slice_bitcast_fusion.2), channel_id=1, source_target_pairs={{0,4},{4,8},{8,12},{12,0},{1,5},{5,9},{9,13},{13,1},{2,6},{6,10},{... | collective-permute-start | bytes 860168 | tf_op jit(solution)/shard_map/ppermute | solution.py:57
  307.9 35.3 %collective-permute-start.35 = (bf16[224,1280]{1,0:T(8,128)(2,1)}, bf16[224,1280]{1,0:T(8,128)(2,1)}, u32[]{:S(2)}, u32[]{:S(2)}) collective-permute-start(bf16[224,1280]{1,0:T(8,128)(2,1)} %fusion.16), channel_id=1, source_target_pairs={{0,4},{4,8},{8,12},{12,0},{1,5},{5,9},{9,13},{13,1},{2,6},{6,10},{... | collective-permute-start | bytes 1720328 | tf_op jit(solution)/shard_map/ppermute | solution.py:57
  336.1 94.6 %collective-permute-start.28 = (bf16[1024,896]{1,0:T(8,128)(2,1)}, bf16[1024,896]{1,0:T(8,128)(2,1)}, u32[]{:S(2)}, u32[]{:S(2)}) collective-permute-start(bf16[1024,896]{1,0:T(8,128)(2,1)} %add_convert_fusion.1), channel_id=1, source_target_pairs={{0,2},{1,3},{2,0},{3,1},{4,6},{5,7},{6,4},{7,5},{8,10},{9,11},{10,... | collective-permute-start | bytes 5505032 | tf_op jit(solution)/shard_map/ppermute | solution.py:53
  339.4 29.7 %collective-permute-start.32 = (bf16[112,1280]{1,0:T(8,128)(2,1)}, bf16[112,1280]{1,0:T(8,128)(2,1)S(1)}, u32[]{:S(2)}, u32[]{:S(2)}) collective-permute-start(bf16[112,1280]{1,0:T(8,128)(2,1)} %dynamic-slice_bitcast_fusion.1), channel_id=1, source_target_pairs={{0,4},{4,8},{8,12},{12,0},{1,5},{5,9},{9,13},{13,1},{2,6},{6,10},{... | collective-permute-start | bytes 860168 | tf_op jit(solution)/shard_map/ppermute | solution.py:57
  343.2 23.6 %collective-permute-start.36 = (bf16[112,1280]{1,0:T(8,128)(2,1)}, bf16[112,1280]{1,0:T(8,128)(2,1)}, u32[]{:S(2)}, u32[]{:S(2)}) collective-permute-start(bf16[112,1280]{1,0:T(8,128)(2,1)} %fusion.27), channel_id=1, source_target_pairs={{0,4},{4,8},{8,12},{12,0},{1,5},{5,9},{9,13},{13,1},{2,6},{6,10},{... | collective-permute-start | bytes 860168 | tf_op jit(solution)/shard_map/ppermute | solution.py:57
  347.3 22.8 %collective-permute-start.37 = (bf16[224,1280]{1,0:T(8,128)(2,1)}, bf16[224,1280]{1,0:T(8,128)(2,1)}, u32[]{:S(2)}, u32[]{:S(2)}) collective-permute-start(bf16[224,1280]{1,0:T(8,128)(2,1)} %fusion.15), channel_id=1, source_target_pairs={{0,16},{16,0},{1,17},{17,1},{2,18},{18,2},{3,19},{19,3},{4,20},{20... | collective-permute-start | bytes 1720328 | tf_op jit(solution)/shard_map/ppermute | solution.py:53
  366.8 41.5 %collective-permute-start.45 = (bf16[224,896]{1,0:T(8,128)(2,1)}, bf16[224,896]{1,0:T(8,128)(2,1)}, u32[]{:S(2)}, u32[]{:S(2)}) collective-permute-start(bf16[224,896]{1,0:T(8,128)(2,1)} %select_bitcast_fusion.1), channel_id=1, source_target_pairs={{0,2},{1,3},{2,0},{3,1},{4,6},{5,7},{6,4},{7,5},{8,10},{9,11},{10,... | collective-permute-start | bytes 1204232 | tf_op jit(solution)/shard_map/ppermute | solution.py:53
  369.1 21.7 %collective-permute-start.38 = (bf16[112,1280]{1,0:T(8,128)(2,1)S(1)}, bf16[112,1280]{1,0:T(8,128)(2,1)}, u32[]{:S(2)}, u32[]{:S(2)}) collective-permute-start(bf16[112,1280]{1,0:T(8,128)(2,1)S(1)} %fusion.25), channel_id=1, source_target_pairs={{0,4},{4,8},{8,12},{12,0},{1,5},{5,9},{9,13},{13,1},{2,6},{6,10},{... | collective-permute-start | bytes 860168 | tf_op jit(solution)/shard_map/ppermute | solution.py:57
  370.0 24.1 %collective-permute-start.39 = (bf16[112,1280]{1,0:T(8,128)(2,1)}, bf16[112,1280]{1,0:T(8,128)(2,1)}, u32[]{:S(2)}, u32[]{:S(2)}) collective-permute-start(bf16[112,1280]{1,0:T(8,128)(2,1)} %fusion.26), channel_id=1, source_target_pairs={{0,4},{4,8},{8,12},{12,0},{1,5},{5,9},{9,13},{13,1},{2,6},{6,10},{... | collective-permute-start | bytes 860168 | tf_op jit(solution)/shard_map/ppermute | solution.py:57
  424.7 23.6 %collective-permute-start.55 = (bf16[112,1280]{1,0:T(8,128)(2,1)S(1)}, bf16[112,1280]{1,0:T(8,128)(2,1)S(1)}, u32[]{:S(2)}, u32[]{:S(2)}) collective-permute-start(bf16[112,1280]{1,0:T(8,128)(2,1)S(1)} %fusion.23), channel_id=1, source_target_pairs={{0,4},{4,8},{8,12},{12,0},{1,5},{5,9},{9,13},{13,1},{2,6},{6,10},{... | collective-permute-start | bytes 860168 | tf_op jit(solution)/shard_map/ppermute | solution.py:57
  (71 other events, 695.2 us)
